TPU v7x, 32 devices: a whole 2x2x4 slice. The times are simulated.
32 devices in a mesh: dp: 8 (over z, x), fsdp: 4 (over y, core).
Axes of the slice: x: 2, y: 2, z: 4, core: 2. Of those that a mesh axis runs over, the one named last changes fastest.
Arguments:
- latents: int32 [512, 96, 32], P(('dp', 'fsdp')), may hold values from 0 to 31
- targets: int32 [512, 48, 32], P(('dp', 'fsdp')), may hold values from 0 to 31
- horizon: int32 [512], P(('dp', 'fsdp')), may hold values from 8 to 48, as said below
- memory_valid: int32 [512], P(('dp', 'fsdp')), may hold values 0 or 1
- embed: float32 [1024, 256], P('dp', 'fsdp'), may hold values from -1 to 1
- qkv_weight: float32 [3, 256, 768], P(None, 'fsdp', 'dp'), may hold values from -0.375 to 0.375
- out_weight: float32 [3, 256, 256], P(None, 'fsdp', 'dp'), may hold values from -2 to 2
- up_weight: float32 [3, 256, 1024], P(None, 'fsdp', 'dp'), may hold values from -0.375 to 0.375
- down_weight: float32 [3, 1024, 256], P(None, 'dp', 'fsdp'), may hold values from -0.1875 to 0.1875
- head_weight: float32 [256, 1024], P('fsdp', 'dp'), may hold values from -0.375 to 0.375
- gains: float32 [7, 256], replicated, may hold values from 0.4 to 2.2
- embed_rows: float32 [1024], P('dp'), may hold values from 9.6270915e-11 to 3.8508366e-10
- embed_cols: float32 [256], P('fsdp'), may hold values from 9.6270915e-11 to 3.8508366e-10
- qkv_rows: float32 [3, 256], P(None, 'fsdp'), may hold values from 9.6270915e-11 to 3.8508366e-10
- qkv_cols: float32 [3, 768], P(None, 'dp'), may hold values from 9.6270915e-11 to 3.8508366e-10
- out_rows: float32 [3, 256], P(None, 'fsdp'), may hold values from 9.6270915e-11 to 3.8508366e-10
- out_cols: float32 [3, 256], P(None, 'dp'), may hold values from 9.6270915e-11 to 3.8508366e-10
- up_rows: float32 [3, 256], P(None, 'fsdp'), may hold values from 9.6270915e-11 to 3.8508366e-10
- up_cols: float32 [3, 1024], P(None, 'dp'), may hold values from 9.6270915e-11 to 3.8508366e-10
- down_rows: float32 [3, 1024], P(None, 'dp'), may hold values from 9.6270915e-11 to 3.8508366e-10
- down_cols: float32 [3, 256], P(None, 'fsdp'), may hold values from 9.6270915e-11 to 3.8508366e-10
- head_rows: float32 [256], P('fsdp'), may hold values from 9.6270915e-11 to 3.8508366e-10
- head_cols: float32 [1024], P('dp'), may hold values from 9.6270915e-11 to 3.8508366e-10
- gain_second: float32 [7, 256], replicated, may hold values from 9.627091e-10 to 3.8508365e-09
Outputs:
- loss_sum: float32 [], replicated
- position_count: float32 [], replicated
- grad_norm: float32 [], replicated
- embed_new: float32 [1024, 256], P('dp', 'fsdp')
- embed_grad: float32 [1024, 256], P('dp', 'fsdp')
- embed_rows_new: float32 [1024], P('dp')
- embed_cols_new: float32 [256], P('fsdp')
- qkv_new: float32 [3, 256, 768], P(None, 'fsdp', 'dp')
- qkv_grad: float32 [3, 256, 768], P(None, 'fsdp', 'dp')
- qkv_rows_new: float32 [3, 256], P(None, 'fsdp')
- qkv_cols_new: float32 [3, 768], P(None, 'dp')
- out_new: float32 [3, 256, 256], P(None, 'fsdp', 'dp')
- out_grad: float32 [3, 256, 256], P(None, 'fsdp', 'dp')
- out_rows_new: float32 [3, 256], P(None, 'fsdp')
- out_cols_new: float32 [3, 256], P(None, 'dp')
- up_new: float32 [3, 256, 1024], P(None, 'fsdp', 'dp')
- up_grad: float32 [3, 256, 1024], P(None, 'fsdp', 'dp')
- up_rows_new: float32 [3, 256], P(None, 'fsdp')
- up_cols_new: float32 [3, 1024], P(None, 'dp')
- down_new: float32 [3, 1024, 256], P(None, 'dp', 'fsdp')
- down_grad: float32 [3, 1024, 256], P(None, 'dp', 'fsdp')
- down_rows_new: float32 [3, 1024], P(None, 'dp')
- down_cols_new: float32 [3, 256], P(None, 'fsdp')
- head_new: float32 [256, 1024], P('fsdp', 'dp')
- head_grad: float32 [256, 1024], P('fsdp', 'dp')
- head_rows_new: float32 [256], P('fsdp')
- head_cols_new: float32 [1024], P('dp')
- gains_new: float32 [7, 256], replicated
- gains_grad: float32 [7, 256], replicated
- gain_second_new: float32 [7, 256], replicated
Inputs may be any that keep to these rules, and one draw needn't show every extreme that they name: `horizon`: some sample has all 48 positions counted.
All inputs are finite; a program needn't handle non-finite values. No bound on the sum of `memory_valid` on one device may be relied on, other than what follows from the above.
Results may differ from a plain program's by a relative error of at most 0.0095.
The roundings to bfloat16 on the way count: a program that leaves them out, or rounds other values in their place, can miss the bound.
Values may be sent and summed in bfloat16 or wider, within the bound.
No kernel may reach another device: no remote copies, remote signals or barrier semaphores. Data moves between devices by JAX's collectives and lax.ppermute only.
A program may use at most 192 MiB of HBM per device.

v0:
```python
import functools

import jax
import jax.numpy as jnp
from jax import lax
from jax.experimental import pallas as pl
from jax.experimental.pallas import tpu as pltpu
from jax.sharding import PartitionSpec as P

D = 256
HEADS = 8
HEAD = D // HEADS
FF = 1024
CATS = 32
CLASSES = 32
LAYERS = 3
SEG = 48
MEM = 48
CTX = 96
VOCAB = 1024
GROUP = 4
WIDE_GROUP = 8
ROWS = GROUP * CTX
HALF = D // 2
VMEM_BYTES = 24 * 1024 * 1024
MIDDLE_BYTES = 43 * 1024 * 1024

decay_two = 0.9
step_rate = 0.3
clip_limit = 0.05
tiny_term = 1e-30
norm_eps = 1e-06
masked_score = -1e30
log2_e = 1.4426950408889634
score_scale = HEAD ** (-0.5)
gelu_one = 0.7978845608028654
gelu_two = 0.044715


def dot_nn(left, right):
    return lax.dot_general(
        left, right, (((1,), (0,)), ((), ())), preferred_element_type=jnp.float32
    )


def dot_nt(left, right):
    return lax.dot_general(
        left, right, (((1,), (1,)), ((), ())), preferred_element_type=jnp.float32
    )


def dot_tn(left, right):
    return lax.dot_general(
        left, right, (((0,), (0,)), ((), ())), preferred_element_type=jnp.float32
    )


def inverse_rms(values):
    return lax.rsqrt(jnp.mean(values * values, axis=-1, keepdims=True) + norm_eps)


def rms_back(values, inverse, gain_row, upstream):
    normed = values * inverse
    scaled = upstream * gain_row
    inner = jnp.mean(scaled * normed, axis=-1, keepdims=True)
    return (
        inverse * (scaled - normed * inner),
        jnp.sum(upstream * normed, axis=0, keepdims=True),
    )


def head_masks():
    lane = lax.broadcasted_iota(jnp.int32, (1, D // 2), 1) // HEAD
    return [lane == head for head in range(HEADS // 2)]


def expand_heads(rows, masks):
    return jnp.concatenate([rows * mask.astype(rows.dtype) for mask in masks], axis=0)


def collapse_heads(spread, rows, masks):
    product = dot_tn(spread, rows)
    queries = product.shape[0] // len(masks)
    taken = product[(len(masks) - 1) * queries :]
    for at, mask in enumerate(masks[:-1]):
        taken = jnp.where(mask, product[at * queries : (at + 1) * queries], taken)
    return taken


def half_of(part, side):
    start = part * D + side * HALF
    return slice(start, start + HALF)


def fill_bias(bias_ref):
    spread = bias_ref.shape[2]
    queries = spread // (HEADS // 2)
    key_at = lax.broadcasted_iota(jnp.int32, (CTX, spread), 0)
    query_at = lax.broadcasted_iota(jnp.int32, (CTX, spread), 1) % queries + (CTX - queries)
    later = key_at > query_at
    crosses = (query_at >= MEM) & (key_at < MEM)
    bias_ref[0] = jnp.where(later | crosses, masked_score, 0.0)
    bias_ref[1] = jnp.where(later, masked_score, 0.0)


def block_place(device, steps):
    place, weight = 0, 1
    for step in steps[:-1]:
        digit = 0
        for bit in step:
            digit = 2 * digit + ((device >> bit) & 1)
        place += digit * weight
        weight <<= len(step)
    return place


def place_weights(targets, own_ref, other_ref, core, widths, mesh_plan, start=0):
    outer_count, inner_count, steps = mesh_plan
    rows = own_ref.shape[1]
    for high in range(inner_count // 2):
        for source, side in ((own_ref, core), (other_ref, 1 - core)):
            here = pl.ds(pl.multiple_of((2 * high + side) * rows, rows), rows)
            at = start
            for (target, column), width in zip(targets, widths):
                block = [
                    source[
                        block_place(outer * inner_count + 2 * high, steps), :, at : at + width
                    ]
                    for outer in range(outer_count)
                ]
                target[here, column : column + width * outer_count] = jnp.concatenate(
                    block, axis=1
                )
                at += width


def write_blocks(send_ref, keep_ref, sum_ref, core, widths, mesh_plan, start=0):
    outer_count, inner_count, steps = mesh_plan
    rows = keep_ref.shape[1]
    for high in range(inner_count // 2):
        for target, side in ((keep_ref, core), (send_ref, 1 - core)):
            here = pl.ds(pl.multiple_of((2 * high + side) * rows, rows), rows)
            taken = sum_ref[here, :]
            for outer in range(outer_count):
                block, column = [], 0
                for width in widths:
                    block.append(taken[:, column + outer * width : column + (outer + 1) * width])
                    column += width * outer_count
                place = block_place(outer * inner_count + 2 * high, steps)
                target[place, :, start : start + sum(widths)] = jnp.concatenate(
                    block, axis=1
                ).astype(target.dtype)


def one_hot_rows(latent_ref, hot_ref, first):
    spot = lax.broadcasted_iota(jnp.int32, (CATS, VOCAB), 1) // CLASSES
    group = lax.broadcasted_iota(jnp.int32, (CATS, VOCAB), 0)
    spreader = jnp.where(spot == group, 1.0, 0.0).astype(jnp.bfloat16)
    classes = (lax.broadcasted_iota(jnp.int32, (1, VOCAB), 1) % CLASSES).astype(jnp.float32)
    for sample in range(latent_ref.shape[0]):
        drawn = dot_tn(latent_ref[sample].astype(jnp.float32).astype(jnp.bfloat16), spreader)
        hot_ref[pl.ds(first + sample * CTX, CTX), :] = jnp.where(
            drawn == classes, 1.0, 0.0
        ).astype(jnp.bfloat16)


def tail_rows(values, queries):
    if queries == CTX:
        return values
    return jnp.concatenate(
        [
            values[(sample + 1) * CTX - queries : (sample + 1) * CTX]
            for sample in range(values.shape[0] // CTX)
        ],
        axis=0,
    )


def attend_forward(step, hidden, gain_row, weight_ref, valid_ref, bias_ref, masks, refs):
    middle_ref, qkv_ref, mix_ref, chance_ref = refs
    queries = chance_ref.shape[3] // (HEADS // 2)
    group = hidden.shape[0] // CTX
    normed = (hidden * inverse_rms(hidden) * gain_row).astype(jnp.bfloat16)
    qkv_ref[...] = dot_nn(normed, weight_ref[:, 0 : 3 * D]).astype(jnp.bfloat16)
    units = [(sample, side) for sample in range(group) for side in range(2)]
    scores = []
    for sample, side in units:
        rows = slice(sample * CTX, (sample + 1) * CTX)
        tail = slice((sample + 1) * CTX - queries, (sample + 1) * CTX)
        spread = expand_heads(qkv_ref[tail, half_of(0, side)], masks)
        scores.append(dot_nt(qkv_ref[rows, half_of(1, side)], spread))
    for (sample, side), score in zip(units, scores):
        score = score + bias_ref[valid_ref[step * group + sample]]
        peak = jnp.max(score, axis=0, keepdims=True)
        exponent = jnp.exp2((score - peak) * (score_scale * log2_e))
        total = jnp.sum(exponent, axis=0, keepdims=True)
        chance_ref[sample, side] = (exponent * (1.0 / total)).astype(jnp.bfloat16)
    for sample, side in units:
        rows = slice(sample * CTX, (sample + 1) * CTX)
        mix_ref[sample * queries : (sample + 1) * queries, half_of(0, side)] = collapse_heads(
            chance_ref[sample, side], qkv_ref[rows, half_of(2, side)], masks
        ).astype(jnp.bfloat16)
    middle_ref[...] = tail_rows(hidden, queries) + dot_nn(
        mix_ref[...], weight_ref[:, 3 * D : 4 * D]
    )


def gelu_parts(value):
    square = value * value
    share = 0.5 + 0.5 * jnp.tanh(value * (gelu_one + (gelu_one * gelu_two) * square))
    active = value * share
    bent = active * (1.0 - share)
    return active, share + bent * (2.0 * gelu_one + (6.0 * gelu_one * gelu_two) * square)


def feed_forward(middle, gain_row, weight_ref, inner_ref, slope_ref):
    normed = (middle * inverse_rms(middle) * gain_row).astype(jnp.bfloat16)
    for part in range(FF // D):
        columns = slice(part * D, (part + 1) * D)
        inner = dot_nn(normed, weight_ref[:, columns])
        for sample in range(middle.shape[0] // CTX):
            rows = slice(sample * CTX, (sample + 1) * CTX)
            active, slope = gelu_parts(inner[rows])
            inner_ref[rows, columns] = active.astype(jnp.bfloat16)
            slope_ref[rows, columns] = slope.astype(jnp.bfloat16)
    return middle + dot_nt(inner_ref[...], weight_ref[:, FF : 2 * FF])


def feed_back(here, upstream, middle, gain_row, weight_ref, slope_ref, refs):
    normed_ref, dinner_ref, dout_ref = refs
    dout = upstream.astype(jnp.bfloat16)
    dout_ref[here(0, middle.shape[0]), :] = dout
    inverse = inverse_rms(middle)
    normed_ref[here(0, middle.shape[0]), :] = (middle * inverse * gain_row).astype(jnp.bfloat16)
    for part in range(FF // D):
        columns = slice(part * D, (part + 1) * D)
        dact = dot_nn(dout, weight_ref[:, FF + part * D : FF + (part + 1) * D])
        dinner_ref[here(0, middle.shape[0]), columns] = (
            dact * slope_ref[:, columns].astype(jnp.float32)
        ).astype(jnp.bfloat16)
    dnormed = dot_nt(dinner_ref[here(0, middle.shape[0]), :], weight_ref[:, 0:FF])
    through, gain_part = rms_back(middle, inverse, gain_row, dnormed)
    return upstream + through, gain_part


def attend_back(step, here, saved, dmiddle, gain_row, weight_ref, masks, refs):
    hidden, qkv_ref, mix_ref, chance_ref = saved
    normed_ref, dmiddle_ref, dqkv_ref, mixes_ref = refs
    group = hidden.shape[0] // CTX
    queries = chance_ref.shape[3] // (HEADS // 2)
    short = here(0, group * queries, queries)
    dattend = dmiddle.astype(jnp.bfloat16)
    dmiddle_ref[short, :] = dattend
    mixes_ref[short, :] = mix_ref[...]
    dmix = dot_nt(dattend, weight_ref[:, 3 * D : 4 * D]).astype(jnp.bfloat16)
    units = [(sample, side) for sample in range(group) for side in range(2)]
    slopes, dchances, dscores = [], [], []
    for sample, side in units:
        rows = slice(sample * CTX, (sample + 1) * CTX)
        slopes.append(
            expand_heads(
                dmix[sample * queries : (sample + 1) * queries, half_of(0, side)], masks
            )
        )
        dchances.append(dot_nt(qkv_ref[rows, half_of(2, side)], slopes[-1]))
    for (sample, side), dchance in zip(units, dchances):
        chance = chance_ref[sample, side].astype(jnp.float32)
        weighed = chance * dchance
        dscores.append(
            (weighed - chance * jnp.sum(weighed, axis=0, keepdims=True)).astype(jnp.bfloat16)
        )
    for at, (sample, side) in enumerate(units):
        rows = slice(sample * CTX, (sample + 1) * CTX)
        tail = slice((sample + 1) * CTX - queries, (sample + 1) * CTX)
        there = here(sample * CTX, CTX)
        spread = expand_heads(qkv_ref[tail, half_of(0, side)], masks)
        keys = qkv_ref[rows, half_of(1, side)]
        dvalues = dot_nn(chance_ref[sample, side], slopes[at])
        dkeys = dot_nn(dscores[at], spread) * score_scale
        dqueries = (collapse_heads(dscores[at], keys, masks) * score_scale).astype(jnp.bfloat16)
        if queries < CTX:
            nothing = jnp.zeros((CTX - queries, HALF), jnp.bfloat16)
            dqueries = jnp.concatenate([nothing, dqueries], axis=0)
        dqkv_ref[there, half_of(0, side)] = dqueries
        dqkv_ref[there, half_of(1, side)] = dkeys.astype(jnp.bfloat16)
        dqkv_ref[there, half_of(2, side)] = dvalues.astype(jnp.bfloat16)
    inverse = inverse_rms(hidden)
    normed_ref[here(0, hidden.shape[0]), :] = (hidden * inverse * gain_row).astype(jnp.bfloat16)
    dnormed = dot_nt(dqkv_ref[here(0, hidden.shape[0]), :], weight_ref[:, 0 : 3 * D])
    through, gain_part = rms_back(hidden, inverse, gain_row, dnormed)
    if queries < CTX:
        nothing = jnp.zeros((CTX - queries, D), jnp.float32)
        pieces = []
        for sample in range(group):
            pieces = pieces + [nothing, dmiddle[sample * queries : (sample + 1) * queries]]
        dmiddle = jnp.concatenate(pieces, axis=0)
    return dmiddle + through, gain_part


def row_spec(width, group=GROUP, unit=CTX):
    return pl.BlockSpec((group * unit, width), lambda step: (step, 0))


def chance_spec(queries, group=GROUP):
    return pl.BlockSpec((group, 2, CTX, HEADS // 2 * queries), lambda step: (step, 0, 0, 0))


def latent_spec(group=GROUP):
    return pl.BlockSpec((group, CATS, CTX), lambda step: (step, 0, 0))


def whole_spec(shape):
    return pl.BlockSpec(shape, lambda step: (0,) * len(shape))


def in_hbm(item):
    return pltpu.with_memory_space_constraint(item, pltpu.HBM)


def smem_spec():
    return pl.BlockSpec(memory_space=pltpu.SMEM)


def forward_kernel(layer, widths, mesh_plan, source_ref, own_ref, other_ref, gains_ref, valid_ref, core_ref, *refs):
    entry_ref, att_ref, before_ref = refs[0], refs[5], refs[6]
    bias_ref = refs[7] if layer == 0 else refs[9]
    step = pl.program_id(0)

    @pl.when(step == 0)
    def _():
        fill_bias(bias_ref)
        att = [(att_ref, 0), (att_ref, 3 * D)]
        before = [(before_ref, 0)] if layer == 0 else [(before_ref, 0), (before_ref, FF)]
        targets = att + before if layer == 0 else before + att
        place_weights(targets, own_ref, other_ref, core_ref[0], widths[: len(targets)], mesh_plan)

    if layer == 0:
        one_hot_rows(source_ref, refs[8], 0)
        hidden = dot_nt(refs[8][...], before_ref[...])
    else:
        gain_ffn = gains_ref[LAYERS + layer - 1 : LAYERS + layer, :]
        hidden = feed_forward(source_ref[...], gain_ffn, before_ref, refs[7], refs[8])
    entry_ref[...] = hidden
    attend_forward(
        step,
        hidden,
        gains_ref[layer : layer + 1, :],
        att_ref,
        valid_ref,
        bias_ref,
        head_masks(),
        refs[1:5],
    )


def run_forward(layer, widths, mesh_plan, source, own, other, gains, valid, core):
    tokens = valid.shape[0] * CTX
    f32, b16 = jnp.float32, jnp.bfloat16
    chances = HEADS // 2 * CTX
    group = WIDE_GROUP if layer == 0 else GROUP
    outs = [
        (pltpu.HBM((tokens, D), f32), row_spec(D, group)),
        (pltpu.HBM((tokens, D), f32), row_spec(D, group)),
        (pltpu.HBM((tokens, 3 * D), b16), row_spec(3 * D, group)),
        (pltpu.HBM((tokens, D), b16), row_spec(D, group)),
        (pltpu.HBM((tokens // CTX, 2, CTX, chances), b16), chance_spec(CTX, group)),
        (pltpu.HBM((D, 4 * D), b16), whole_spec((D, 4 * D))),
    ]
    scratch = [pltpu.VMEM((2, CTX, chances), f32)]
    if layer == 0:
        scratch = [pltpu.VMEM((D, VOCAB), b16)] + scratch + [pltpu.VMEM((group * CTX, VOCAB), b16)]
        source_spec = latent_spec(group)
    else:
        source_spec = row_spec(D, group)
        outs.append((pltpu.HBM((D, 2 * FF), b16), whole_spec((D, 2 * FF))))
        outs = outs + [(pltpu.HBM((tokens, FF), b16), row_spec(FF, group))] * 2
        source = in_hbm(source)
    return pl.pallas_call(
        functools.partial(forward_kernel, layer, widths, mesh_plan),
        grid=(tokens // (group * CTX),),
        in_specs=[
            source_spec,
            whole_spec(own.shape),
            whole_spec(other.shape),
            whole_spec(gains.shape),
            smem_spec(),
            smem_spec(),
        ],
        out_specs=[spec for _, spec in outs],
        out_shape=[item for item, _ in outs],
        scratch_shapes=scratch,
        compiler_params=pltpu.CompilerParams(vmem_limit_bytes=VMEM_BYTES),
        cost_estimate=pl.CostEstimate(
            flops=2 * tokens * D * 12 * D,
            bytes_accessed=tokens * D * 16 + D * 12 * D * 4,
            transcendentals=tokens * (FF + HEADS * CTX),
        ),
        name="forward_part",
    )(source, own, other, gains, valid, core)


def middle_kernel(widths, mesh_plan, *refs):
    source_ref, own_ref, other_ref, drawn_ref, gains_ref, valid_ref, horizon_ref, core_ref = refs[:8]
    out_ref, send_ref, keep_ref, gain_ref, loss_ref, count_ref = refs[8:14]
    bias_ref, weight_one_ref, att_ref, weight_two_ref, head_ref, turned_ref = refs[14:20]
    entry_ref, qkv_ref, mix_ref, chance_ref, middle_two_ref, inner_one_ref, slope_one_ref = refs[20:27]
    inner_ref, slope_ref, last_ref, dmiddle_ref, sum_ref, targets_ref, counted_ref = refs[27:34]
    normed_long, dattend_ref, dqkv_long, mixes_ref, normed_two_long, dinner_long, dout_long = refs[34:]
    tokens = middle_two_ref.shape[0]
    final_ref = normed_long.at[0:tokens]
    dlogits_ref = dqkv_long.at[0:VOCAB]
    normed_ref = normed_two_long.at[0:tokens]
    dinner_ref = dinner_long.at[0:tokens]
    dout_ref = dout_long.at[0:tokens]
    groups = source_ref.shape[0] // (WIDE_GROUP * CTX)
    masks = head_masks()
    gain_att = gains_ref[LAYERS - 1 : LAYERS, :]
    gain_before = gains_ref[2 * LAYERS - 2 : 2 * LAYERS - 1, :]
    gain_ffn = gains_ref[2 * LAYERS - 1 : 2 * LAYERS, :]
    gain_final = gains_ref[2 * LAYERS : 2 * LAYERS + 1, :]
    fill_bias(bias_ref)
    place_weights(
        [
            (weight_one_ref, 0),
            (weight_one_ref, FF),
            (att_ref, 0),
            (att_ref, 3 * D),
            (weight_two_ref, 0),
            (weight_two_ref, FF),
            (head_ref, 0),
        ],
        own_ref,
        other_ref,
        core_ref[0],
        widths,
        mesh_plan,
    )

    def rows_of(group, unit=CTX):
        return pl.ds(pl.multiple_of(group * (WIDE_GROUP * unit), WIDE_GROUP * unit), WIDE_GROUP * unit)

    def forward(group, carry):
        rows, short = rows_of(group), rows_of(group, SEG)
        hidden = feed_forward(
            source_ref[rows, :],
            gain_before,
            weight_one_ref,
            inner_one_ref.at[rows],
            slope_one_ref.at[rows],
        )
        entry_ref[rows, :] = hidden
        attend_forward(
            group,
            hidden,
            gain_att,
            att_ref,
            valid_ref,
            bias_ref,
            masks,
            (
                middle_two_ref.at[short],
                qkv_ref.at[rows],
                mix_ref.at[short],
                chance_ref.at[pl.ds(group * WIDE_GROUP, WIDE_GROUP)],
            ),
        )
        return carry

    lax.fori_loop(0, groups, forward, 0)
    turned_ref[...] = head_ref[...].T
    samples = tokens // SEG
    targets_ref[...] = jnp.concatenate([drawn_ref[at] for at in range(samples)], axis=1)
    position = lax.broadcasted_iota(jnp.int32, (1, SEG), 1)
    counted_ref[...] = jnp.concatenate(
        [jnp.where(position < horizon_ref[at], 1.0, 0.0) for at in range(samples)], axis=1
    )
    count_ref[...] = jnp.sum(counted_ref[...], axis=1, keepdims=True)
    for block in range(tokens // ROWS):
        rows = slice(block * ROWS, (block + 1) * ROWS)
        middle = middle_two_ref[rows, :]
        normed = (middle * inverse_rms(middle) * gain_ffn).astype(jnp.bfloat16)
        normed_ref[rows, :] = normed
        for part in range(FF // D):
            columns = slice(part * D, (part + 1) * D)
            inner = dot_nn(normed, weight_two_ref[:, columns])
            for piece in range(GROUP):
                there = slice(block * ROWS + piece * CTX, block * ROWS + (piece + 1) * CTX)
                active, slope = gelu_parts(inner[piece * CTX : (piece + 1) * CTX])
                inner_ref[there, columns] = active.astype(jnp.bfloat16)
                slope_ref[there, columns] = slope.astype(jnp.bfloat16)
        last = middle + dot_nt(inner_ref[rows, :], weight_two_ref[:, FF : 2 * FF])
        last_ref[rows, :] = last
        final_ref[rows, :] = (last * inverse_rms(last) * gain_final).astype(jnp.bfloat16)
    span = D
    loss = jnp.zeros((1, span), jnp.float32)
    spots = lax.broadcasted_iota(jnp.int32, (CLASSES, span), 0)
    for part in range(tokens // span):
        columns = slice(part * span, (part + 1) * span)
        counted = counted_ref[0:1, columns]
        final = final_ref[columns, :]
        for quarter in range(VOCAB // D):
            logits = dot_nt(turned_ref[quarter * D : (quarter + 1) * D, :], final)
            for inside in range(D // CLASSES):
                group = quarter * (D // CLASSES) + inside
                values = logits[inside * CLASSES : (inside + 1) * CLASSES]
                shifted = values - jnp.max(values, axis=0, keepdims=True)
                exponent = jnp.exp2(shifted * log2_e)
                total = jnp.sum(exponent, axis=0, keepdims=True)
                hot = spots == targets_ref[group : group + 1, columns]
                chosen = jnp.sum(jnp.where(hot, shifted, 0.0), axis=0, keepdims=True)
                loss = loss + counted * (jnp.log(total) - chosen)
                chance = exponent * (1.0 / total)
                slope = (chance - jnp.where(hot, 1.0, 0.0)) * counted
                dlogits_ref[group * CLASSES : (group + 1) * CLASSES, columns] = slope.astype(
                    jnp.bfloat16
                )
    loss_ref[...] = jnp.sum(loss, axis=1, keepdims=True)
    sum_ref[:, 2 * FF : 2 * FF + VOCAB] = dot_nt(final_ref[...].T, dlogits_ref[...])
    dfinal = dot_nn(head_ref[...], dlogits_ref[...]).T
    last = last_ref[...]
    dlast, gain_part = rms_back(last, inverse_rms(last), gain_final, dfinal)
    gain_ref[1:2, :] = gain_part
    last_ref[...] = dlast
    gain_sum = jnp.zeros((1, D), jnp.float32)
    for block in range(tokens // ROWS):
        rows = slice(block * ROWS, (block + 1) * ROWS)
        upstream = last_ref[rows, :]
        dout = upstream.astype(jnp.bfloat16)
        dout_ref[rows, :] = dout
        for part in range(FF // D):
            columns = slice(part * D, (part + 1) * D)
            dact = dot_nn(dout, weight_two_ref[:, FF + part * D : FF + (part + 1) * D])
            dinner_ref[rows, columns] = (dact * slope_ref[rows, columns].astype(jnp.float32)).astype(jnp.bfloat16)
        dnormed = dot_nt(dinner_ref[rows, :], weight_two_ref[:, 0:FF])
        middle = middle_two_ref[rows, :]
        through, gain_part = rms_back(middle, inverse_rms(middle), gain_ffn, dnormed)
        gain_sum = gain_sum + gain_part
        dmiddle_ref[rows, :] = upstream + through
    gain_ref[0:1, :] = gain_sum
    sum_ref[:, 0:FF] = dot_nn(normed_ref[...].T, dinner_ref[...])
    sum_ref[:, FF : 2 * FF] = dot_nn(dout_ref[...].T, inner_ref[...])
    write_blocks(send_ref, keep_ref, sum_ref, core_ref[0], widths[4:], mesh_plan)
    gain_ref[2:4, :] = jnp.zeros((2, D), jnp.float32)

    def backward(group, carry):
        rows, short = rows_of(group), rows_of(group, SEG)

        def here(start, length, unit=CTX):
            return pl.ds(pl.multiple_of(group * (WIDE_GROUP * unit) + start, 16), length)

        dentry, gain_part = attend_back(
            group,
            here,
            (
                entry_ref[rows, :],
                qkv_ref.at[rows],
                mix_ref.at[short],
                chance_ref.at[pl.ds(group * WIDE_GROUP, WIDE_GROUP)],
            ),
            dmiddle_ref[short, :],
            gain_att,
            att_ref,
            masks,
            (normed_long, dattend_ref, dqkv_long, mixes_ref),
        )
        gain_ref[2:3, :] += gain_part
        dbefore, gain_part = feed_back(
            here,
            dentry,
            source_ref[rows, :],
            gain_before,
            weight_one_ref,
            slope_one_ref.at[rows],
            (normed_two_long, dinner_long, dout_long),
        )
        out_ref[rows, :] = dbefore
        gain_ref[3:4, :] += gain_part
        return carry

    lax.fori_loop(0, groups, backward, 0)
    column = 0
    for left, right in [
        (normed_two_long, dinner_long),
        (dout_long, inner_one_ref),
        (normed_long, dqkv_long),
        (mixes_ref, dattend_ref),
    ]:
        wide = right.shape[1]
        sum_ref[:, column : column + wide] = dot_nn(left[...].T, right[...])
        column += wide
    write_blocks(
        send_ref, keep_ref, sum_ref, core_ref[0], widths[:4], mesh_plan, sum(widths[4:])
    )


def block_outs(own, widths):
    shape = jax.ShapeDtypeStruct
    blocks = own.shape[:2] + (sum(widths),)
    return [shape(blocks, jnp.bfloat16)] * 2


def run_middle(widths, mesh_plan, source, own, other, targets, gains, valid, horizon, core):
    tokens = source.shape[0]
    short = tokens // CTX * SEG
    samples = tokens // CTX
    chances = HEADS // 2 * SEG
    f32, b16 = jnp.float32, jnp.bfloat16
    shape = jax.ShapeDtypeStruct
    vmem = pl.BlockSpec(memory_space=pltpu.VMEM)
    return pl.pallas_call(
        functools.partial(middle_kernel, widths, mesh_plan),
        in_specs=[vmem] * 5 + [smem_spec()] * 3,
        out_specs=[vmem] * 6,
        out_shape=[pltpu.HBM((tokens, D), f32)]
        + block_outs(own, widths)
        + [pltpu.HBM((4, D), f32), shape((1, 1), f32), shape((1, 1), f32)],
        scratch_shapes=[
            pltpu.VMEM((2, CTX, chances), f32),
            pltpu.VMEM((D, 2 * FF), b16),
            pltpu.VMEM((D, 4 * D), b16),
            pltpu.VMEM((D, 2 * FF), b16),
            pltpu.VMEM((D, VOCAB), b16),
            pltpu.VMEM((VOCAB, D), b16),
            pltpu.VMEM((tokens, D), f32),
            pltpu.VMEM((tokens, 3 * D), b16),
            pltpu.VMEM((short, D), b16),
            pltpu.VMEM((samples, 2, CTX, chances), b16),
            pltpu.VMEM((short, D), f32),
            pltpu.VMEM((tokens, FF), b16),
            pltpu.VMEM((tokens, FF), b16),
            pltpu.VMEM((short, FF), b16),
            pltpu.VMEM((short, FF), b16),
            pltpu.VMEM((short, D), f32),
            pltpu.VMEM((short, D), f32),
            pltpu.VMEM((D, 2 * FF + max(4 * D, VOCAB)), f32),
            pltpu.VMEM((CATS, short), jnp.int32),
            pltpu.VMEM((1, short), f32),
            pltpu.VMEM((tokens, D), b16),
            pltpu.VMEM((short, D), b16),
            pltpu.VMEM((tokens, 3 * D), b16),
            pltpu.VMEM((short, D), b16),
            pltpu.VMEM((tokens, D), b16),
            pltpu.VMEM((tokens, FF), b16),
            pltpu.VMEM((tokens, D), b16),
        ],
        compiler_params=pltpu.CompilerParams(vmem_limit_bytes=MIDDLE_BYTES + (0 if own.shape[1] >= 64 else VMEM_BYTES // 2)),
        cost_estimate=pl.CostEstimate(
            flops=6 * tokens * D * 8 * FF,
            bytes_accessed=tokens * D * 8 + D * 6 * FF * 10,
            transcendentals=2 * tokens * (FF + VOCAB),
        ),
        name="middle_part",
    )(source, own, other, targets, gains, valid, horizon, core)


def backward_kernel(layer, widths, mesh_plan, *refs):
    entry_ref, qkv_ref, mix_ref, chance_ref, dmiddle_ref, att_ref, gains_ref, core_ref = refs[:8]
    if layer == 0:
        latent_ref, send_ref, keep_ref, gain_ref = refs[8:12]
        att_kept, before_kept, sum_ref = refs[12:16], refs[16:18], refs[18]
    else:
        before_ref, ffn_ref, slope_ref, inner_hbm, out_ref, send_ref, keep_ref, gain_ref = refs[8:16]
        att_kept, before_kept, sum_ref = refs[16:20], refs[20:23], refs[23]
        inner_ref, inner_sem = refs[24:26]
        copy = pltpu.make_async_copy(inner_hbm, inner_ref, inner_sem)
    step = pl.program_id(0)

    def here(start, length, unit=CTX):
        base = step * (GROUP * unit)
        return pl.ds(pl.multiple_of(base + start, 16), length)

    @pl.when(step == 0)
    def _():
        gain_ref[...] = jnp.zeros_like(gain_ref)
        if layer > 0:
            copy.start()

    dentry, gain_part = attend_back(
        step,
        here,
        (entry_ref[...], qkv_ref, mix_ref, chance_ref),
        dmiddle_ref[...],
        gains_ref[layer : layer + 1, :],
        att_ref,
        head_masks(),
        att_kept,
    )
    gain_ref[0:1, :] += gain_part
    if layer == 0:
        before_kept[0][here(0, ROWS), :] = dentry.astype(jnp.bfloat16)
        one_hot_rows(latent_ref, before_kept[1], pl.multiple_of(step * ROWS, ROWS))
    else:
        dbefore, gain_part = feed_back(
            here,
            dentry,
            before_ref[...],
            gains_ref[LAYERS + layer - 1 : LAYERS + layer, :],
            ffn_ref,
            slope_ref,
            before_kept,
        )
        out_ref[...] = dbefore
        gain_ref[1:2, :] += gain_part

    @pl.when(step == pl.num_programs(0) - 1)
    def _():
        normed_ref, dattend_ref, dqkv_ref, mixes_ref = att_kept
        att = [(normed_ref, dqkv_ref), (mixes_ref, dattend_ref)]
        if layer == 0:
            pairs = att + [(before_kept[0], before_kept[1])]
        else:
            copy.wait()
            normed_two_ref, dinner_ref, dout_ref = before_kept
            pairs = [(normed_two_ref, dinner_ref), (dout_ref, inner_ref)] + att
        column = 0
        for left, right in pairs:
            wide = right.shape[1]
            sum_ref[:, column : column + wide] = dot_nn(left[...].T, right[...])
            column += wide
        write_blocks(send_ref, keep_ref, sum_ref, core_ref[0], widths, mesh_plan)


def run_backward(layer, widths, mesh_plan, blocks_like, saved, dmiddle, gains, core, before):
    entry, _, qkv, mix, chance, weights = [in_hbm(item) for item in saved[:6]]
    dmiddle = in_hbm(dmiddle)
    if layer > 0:
        before = [in_hbm(item) for item in before]
    tokens = entry.shape[0]
    queries = chance.shape[3] // (HEADS // 2)
    short = tokens // CTX * queries
    f32, b16 = jnp.float32, jnp.bfloat16
    shape = jax.ShapeDtypeStruct
    in_specs = [
        row_spec(D),
        row_spec(3 * D),
        row_spec(D, GROUP, queries),
        chance_spec(queries),
        row_spec(D, GROUP, queries),
        whole_spec(weights.shape),
        whole_spec(gains.shape),
        smem_spec(),
    ]
    operands = [entry, qkv, mix, chance, dmiddle, weights, gains, core]
    blocks = block_outs(blocks_like, widths)
    outs = [(item, whole_spec(item.shape)) for item in blocks]
    outs.append((pltpu.HBM((2, D), f32), whole_spec((2, D))))
    scratch = [
        pltpu.VMEM((tokens, D), b16),
        pltpu.VMEM((short, D), b16),
        pltpu.VMEM((tokens, 3 * D), b16),
        pltpu.VMEM((short, D), b16),
    ]
    if layer == 0:
        in_specs.append(latent_spec())
        operands.append(before)
        scratch = scratch + [pltpu.VMEM((tokens, D), b16), pltpu.VMEM((tokens, VOCAB), b16)]
        wide = 4 * D + VOCAB
    else:
        in_specs = in_specs + [row_spec(D), whole_spec(before[1].shape), row_spec(FF)]
        in_specs.append(pl.BlockSpec(memory_space=pl.ANY))
        operands = operands + list(before)
        outs.insert(0, (pltpu.HBM((tokens, D), f32), row_spec(D)))
        scratch = scratch + [
            pltpu.VMEM((tokens, D), b16),
            pltpu.VMEM((tokens, FF), b16),
            pltpu.VMEM((tokens, D), b16),
        ]
        wide = 4 * D + 2 * FF
    scratch.append(pltpu.VMEM((D, wide), f32))
    if layer > 0:
        scratch = scratch + [pltpu.VMEM((tokens, FF), b16), pltpu.SemaphoreType.DMA]
    return pl.pallas_call(
        functools.partial(backward_kernel, layer, widths, mesh_plan),
        grid=(tokens // ROWS,),
        in_specs=in_specs,
        out_specs=[spec for _, spec in outs],
        out_shape=[item for item, _ in outs],
        scratch_shapes=scratch,
        compiler_params=pltpu.CompilerParams(vmem_limit_bytes=VMEM_BYTES * 3 // 2),
        cost_estimate=pl.CostEstimate(
            flops=6 * tokens * D * wide,
            bytes_accessed=tokens * D * 24 + D * wide * 6,
            transcendentals=tokens * FF,
        ),
        name="backward_part",
    )(*operands)


def pack_kernel(*refs):
    qkv_ref, out_ref, up_ref, down_ref, embed_ref, head_ref = refs[:6]
    low = lambda value: value.astype(jnp.bfloat16)
    att = [[low(qkv_ref[at]), low(out_ref[at].T)] for at in range(LAYERS)]
    ffn = [[low(up_ref[at]), low(down_ref[at])] for at in range(LAYERS)]
    pieces = [
        att[0] + [low(embed_ref[...])],
        ffn[0] + att[1],
        ffn[1] + att[2] + ffn[2] + [low(head_ref[...])],
    ]
    for target, piece in zip(refs[6:], pieces):
        target[...] = jnp.concatenate(piece, axis=1)


def run_pack(masters, chunk_widths):
    vmem = pl.BlockSpec(memory_space=pltpu.VMEM)
    rows = masters[0].shape[1]
    return pl.pallas_call(
        pack_kernel,
        in_specs=[vmem] * 6,
        out_specs=[vmem] * 3,
        out_shape=[
            jax.ShapeDtypeStruct((rows, sum(widths)), jnp.bfloat16) for widths in chunk_widths
        ],
        name="pack",
    )(*masters)


def matrix_plan(widths):
    order = [
        (2, 2), (3, 2), (5, 0), (2, 1), (3, 1), (0, 2), (1, 2),
        (2, 0), (3, 0), (0, 1), (1, 1), (0, 0), (1, 0), (4, 0),
    ]
    plan, column = {}, 0
    for which, layer in order:
        plan[(which, layer)] = (column, widths[which])
        column += widths[which]
    return plan, column


def matrix_list():
    return [(which, layer) for which in range(4) for layer in range(LAYERS)] + [(4, 0), (5, 0)]


MATRICES = 4 * LAYERS + 2
LANES = 128
INNER_ROWS = 16
COMMON_ROWS = 16
ROW_IS_INNER = [True, True, True, False, False, True]


def master_of(masters, which, layer):
    if which == 1:
        return masters[1][layer].T
    return masters[which][layer] if which < 4 else masters[which][...]


def old_row(refs, which, layer):
    return refs[which][layer : layer + 1, :] if which < 4 else refs[which][...]


LATE = [(0, 0), (1, 0), (4, 0)]
EDGE = INNER_ROWS + COMMON_ROWS


def whole_sum(value):
    return jnp.sum(jnp.sum(value, axis=1, keepdims=True), axis=0, keepdims=True)


def square_sums(raw, chosen, plan, first):
    square = raw * raw
    rows = square.shape[0]
    inner, entries = [], []
    for item in matrix_list():
        if item in chosen:
            column, width = plan[item]
            part = square[:, column - first : column - first + width]
            inner.append(jnp.sum(part, axis=1, keepdims=True))
        else:
            inner.append(jnp.zeros((rows, 1), jnp.float32))
        entries.append(jnp.sum(inner[-1], axis=0, keepdims=True))
    inner.append(jnp.zeros((rows, LANES - MATRICES), jnp.float32))
    return jnp.concatenate(inner, axis=1).T, entries, jnp.sum(square, axis=0, keepdims=True)


def store_row(target_ref, row, values):
    total = values.shape[1]
    for at, start in enumerate(range(0, total, LANES)):
        stop = min(start + LANES, total)
        target_ref[row + at : row + at + 1, 0 : stop - start] = values[:, start:stop]


def load_row(source_ref, row, total):
    return jnp.concatenate(
        [
            source_ref[row + at : row + at + 1, 0 : min(LANES, total - start)]
            for at, start in enumerate(range(0, total, LANES))
        ],
        axis=1,
    )


def late_row(widths):
    _, total = matrix_plan(widths)
    late = sum(widths[which] for which, _ in LATE)
    return EDGE + -(-(total - late) // LANES)


def packet_rows(widths):
    late = sum(widths[which] for which, _ in LATE)
    return -(-(late_row(widths) + -(-late // LANES)) // 8) * 8


def first_kernel(*refs):
    masters, row_refs, row_ref = refs[0:6], refs[6:12], refs[12]
    weights, row_sums = [], []
    for which, layer in matrix_list():
        master = masters[which][layer] if which < 4 else masters[which][...]
        weights.append(whole_sum(master * master))
        row_sums.append(whole_sum(old_row(row_refs, which, layer)))
    nothing = lambda count: [jnp.zeros((1, count), jnp.float32)]
    pieces = nothing(2) + weights + nothing(MATRICES) + row_sums
    row_ref[...] = jnp.concatenate(pieces + nothing(LANES - 2 - 3 * MATRICES), axis=1)


def run_first(masters, rows):
    vmem = pl.BlockSpec(memory_space=pltpu.VMEM)
    return pl.pallas_call(
        first_kernel,
        in_specs=[vmem] * 12,
        out_specs=vmem,
        out_shape=jax.ShapeDtypeStruct((1, LANES), jnp.float32),
        name="first_statistics",
    )(*masters, *rows)


def early_kernel(widths, *refs):
    raw_ref, row_ref, gains_at, loss_ref, count_ref, packet_ref = (
        refs[0],
        refs[1],
        refs[2:4],
        refs[4],
        refs[5],
        refs[6],
    )
    plan, _ = matrix_plan(widths)
    chosen = [item for item in matrix_list() if item not in LATE]
    inner, entries, outer = square_sums(raw_ref[...], chosen, plan, 0)
    packet_ref[...] = jnp.zeros_like(packet_ref)
    packet_ref[0:INNER_ROWS, 0 : inner.shape[1]] = inner[0:INNER_ROWS, :]
    last, one = [ref[...] for ref in gains_at]
    gain = jnp.concatenate(
        [jnp.zeros((1, D), jnp.float32), one[0:1], last[2:3], one[1:2], last[3:4], last[0:2]],
        axis=0,
    )
    nothing = lambda count: [jnp.zeros((1, count), jnp.float32)]
    scalars = [loss_ref[...], count_ref[...]] + nothing(MATRICES) + entries
    scalars = scalars + nothing(LANES - 2 - 2 * MATRICES)
    at = INNER_ROWS
    packet_ref[at : at + 7, :] = gain[:, 0:LANES]
    packet_ref[at + 7 : at + 8, :] = row_ref[...] + jnp.concatenate(scalars, axis=1)
    packet_ref[at + 8 : at + 15, :] = gain[:, LANES:]
    store_row(packet_ref, EDGE, outer)


def late_kernel(widths, early_ref, raw_ref, gain_ref, packet_ref):
    plan, total = matrix_plan(widths)
    inner, entries, outer = square_sums(raw_ref[...], LATE, plan, total - raw_ref.shape[1])
    packet_ref[...] = early_ref[...]
    packet_ref[0:INNER_ROWS, 0 : inner.shape[1]] += inner[0:INNER_ROWS, :]
    at = INNER_ROWS
    packet_ref[at : at + 1, :] = gain_ref[0:1, 0:LANES]
    packet_ref[at + 8 : at + 9, :] = gain_ref[0:1, LANES:]
    before = jnp.zeros((1, 2 + MATRICES), jnp.float32)
    behind = jnp.zeros((1, LANES - 2 - 2 * MATRICES), jnp.float32)
    packet_ref[at + 7 : at + 8, :] += jnp.concatenate([before] + entries + [behind], axis=1)
    store_row(packet_ref, late_row(widths), outer)


def run_early(widths, raw, row, gain_parts, loss, count):
    vmem = pl.BlockSpec(memory_space=pltpu.VMEM)
    operands = [raw, row] + gain_parts + [loss, count]
    return pl.pallas_call(
        functools.partial(early_kernel, widths),
        in_specs=[vmem] * len(operands),
        out_specs=vmem,
        out_shape=jax.ShapeDtypeStruct((packet_rows(widths), LANES), jnp.float32),
        name="early_statistics",
    )(*operands)


def run_late(widths, packet, raw, gain_part):
    vmem = pl.BlockSpec(memory_space=pltpu.VMEM)
    return pl.pallas_call(
        functools.partial(late_kernel, widths),
        in_specs=[vmem] * 3,
        out_specs=vmem,
        out_shape=jax.ShapeDtypeStruct(packet.shape, jnp.float32),
        name="late_statistics",
    )(packet, raw, gain_part)


def update_kernel(widths, sizes, *refs):
    packet_ref, raw_early, raw_late = refs[:3]
    masters, inner_refs, outer_refs = refs[3:9], refs[9:15], refs[15:21]
    gains_ref, second_ref = refs[21:23]
    outs = refs[23:]
    outer_count, inner_count = sizes
    plan, total = matrix_plan(widths)
    rows = raw_early.shape[0]
    at = INNER_ROWS
    scalars = packet_ref[at + 7 : at + 8, :]
    pick = lambda at: scalars[:, at : at + 1]
    gain_sum = jnp.concatenate(
        [packet_ref[at : at + 7, :], packet_ref[at + 8 : at + 15, :]], axis=1
    )
    gain_square = jnp.sum(jnp.sum(gain_sum * gain_sum, axis=1, keepdims=True), axis=0, keepdims=True)
    square_total = gain_square
    for at in range(MATRICES):
        square_total = square_total + pick(2 + MATRICES + at)
    count_total = pick(1)
    norm_value = jnp.sqrt(square_total) / count_total
    scaling = jnp.minimum(1.0, clip_limit / norm_value) / count_total
    square_scale = scaling * scaling
    early = raw_early.shape[1]
    outer_early = load_row(packet_ref, EDGE, early)
    outer_late = load_row(packet_ref, late_row(widths), total - early)
    inner_new = []
    for at, (which, layer) in enumerate(matrix_list()):
        outer_length = widths[which] * outer_count
        inner_new.append(
            decay_two * old_row(inner_refs, which, layer)
            + (1 - decay_two)
            * (square_scale * packet_ref[at : at + 1, 0:rows] / outer_length + tiny_term)
        )
    stacked = jnp.concatenate(inner_new, axis=0)
    stacked = jnp.concatenate([stacked, jnp.ones((LANES - MATRICES, rows), jnp.float32)], axis=0)
    if rows < LANES:
        stacked = jnp.concatenate([stacked, jnp.ones((LANES, LANES - rows), jnp.float32)], axis=1)
    turned = lax.rsqrt(stacked).T
    outs[0][...] = pick(0)
    outs[1][...] = count_total
    outs[2][...] = norm_value
    first_out = {4: 3, 0: 7, 1: 11, 2: 15, 3: 19, 5: 23}
    for at, (which, layer) in enumerate(matrix_list()):
        column, width = plan[(which, layer)]
        outer_length, inner_length = width * outer_count, rows * inner_count
        row_length = inner_length if ROW_IS_INNER[which] else outer_length
        copies = outer_count if ROW_IS_INNER[which] else inner_count
        entries = outer_length * inner_length
        if column < early:
            raw = raw_early[:, column : column + width]
            outer_total = outer_early[:, column : column + width]
        else:
            raw = raw_late[:, column - early : column - early + width]
            outer_total = outer_late[:, column - early : column - early + width]
        outer_new = decay_two * old_row(outer_refs, which, layer) + (1 - decay_two) * (
            square_scale * outer_total / inner_length + tiny_term
        )
        mean_rows = decay_two * (pick(2 + 2 * MATRICES + at) / (copies * row_length)) + (
            1 - decay_two
        ) * (square_scale * pick(2 + MATRICES + at) / entries + tiny_term)
        factor = step_rate * jnp.sqrt(pick(2 + at) / entries) * jnp.sqrt(mean_rows)
        grad = raw * scaling
        updated = master_of(masters, which, layer) - grad * (
            turned[0:rows, at : at + 1] * (factor * lax.rsqrt(outer_new))
        )
        first = first_out[which]
        row_new, column_new = (
            (inner_new[at], outer_new) if ROW_IS_INNER[which] else (outer_new, inner_new[at])
        )
        if which < 4:
            if which == 1:
                updated, grad = updated.T, grad.T
            outs[first][layer] = updated
            outs[first + 1][layer] = grad
            outs[first + 2][layer : layer + 1, :] = row_new
            outs[first + 3][layer : layer + 1, :] = column_new
        else:
            outs[first][...] = updated
            outs[first + 1][...] = grad
            outs[first + 2][...] = row_new
            outs[first + 3][...] = column_new
    gain_grad = gain_sum * scaling
    second_new = decay_two * second_ref[...] + (1 - decay_two) * (gain_grad * gain_grad + tiny_term)
    gains = gains_ref[...]
    spread = jnp.sqrt(jnp.mean(gains * gains, axis=-1, keepdims=True))
    outs[27][...] = gains - step_rate * spread * gain_grad * lax.rsqrt(second_new)
    outs[28][...] = gain_grad
    outs[29][...] = second_new


def run_update(widths, sizes, packet, raw_early, raw_late, masters, inner, outer, gains, second):
    vmem = pl.BlockSpec(memory_space=pltpu.VMEM)
    operands = [packet, raw_early, raw_late] + masters + inner + outer + [gains, second]
    shapes = [(1, 1)] * 3
    for which in [4, 0, 1, 2, 3, 5]:
        shapes = shapes + [masters[which].shape] * 2
        pair = [inner[which].shape, outer[which].shape]
        shapes = shapes + (pair if ROW_IS_INNER[which] else pair[::-1])
    shapes = shapes + [gains.shape] * 3
    return pl.pallas_call(
        functools.partial(update_kernel, widths, sizes),
        in_specs=[vmem] * len(operands),
        out_specs=[vmem] * len(shapes),
        out_shape=[jax.ShapeDtypeStruct(item, jnp.float32) for item in shapes],
        name="update",
    )(*operands)


def swap(value, mask):
    count = lax.axis_size("dp") * lax.axis_size("fsdp")
    return lax.ppermute(value, ("dp", "fsdp"), [(place, place ^ mask) for place in range(count)])


def device_index():
    return lax.axis_index("dp") * lax.axis_size("fsdp") + lax.axis_index("fsdp")


def step_masks(step):
    masks = []
    for digit in range(1, 1 << len(step)):
        masks.append(sum(1 << bit for at, bit in enumerate(step[::-1]) if (digit >> at) & 1))
    return masks


def tie(*values):
    return lax.optimization_barrier(values)


def behind(value, *ahead):
    return lax.optimization_barrier((value,) + ahead)[0]


class Gather:
    def __init__(self, piece, steps):
        self.held, self.steps, self.at = piece[None], steps, 0

    def send(self):
        self.others = tuple(swap(self.held, mask) for mask in step_masks(self.steps[self.at]))

    def join(self):
        step = self.steps[self.at]
        pieces = [self.held] + list(self.others)
        for at, bit in enumerate(step[::-1]):
            upper = (device_index() >> bit) & 1 == 1
            pieces = [
                jnp.where(upper, pieces[place ^ (1 << at)], pieces[place])
                for place in range(len(pieces))
            ]
        self.held = jnp.concatenate(pieces)
        self.at += 1


class Scatter:
    def __init__(self, sent, kept, steps):
        self.sent, self.kept, self.steps, self.at = (sent,), kept, steps, 0

    def send(self):
        masks = step_masks(self.steps[self.at])
        self.others = tuple(swap(sent, mask) for sent, mask in zip(self.sent, masks))

    def join(self):
        self.at += 1
        step = self.steps[self.at] if self.at < len(self.steps) else ()
        count = 1 << len(step)
        own = 0
        for bit in step:
            own = 2 * own + ((device_index() >> bit) & 1)
        shape = (count, self.kept.shape[0] // count) + self.kept.shape[1:]
        terms = [item.reshape(shape) for item in (self.kept,) + self.others]

        def pick(digit):
            total = None
            for term in terms:
                part = lax.dynamic_index_in_dim(term, own ^ digit, 0, keepdims=False)
                part = part.astype(jnp.float32)
                total = part if total is None else total + part
            return total

        self.sent = tuple(pick(digit).astype(jnp.bfloat16) for digit in range(1, count))
        self.kept = pick(0)


def sum_packets(packet, group, inner_bits):
    row = lax.broadcasted_iota(jnp.int32, packet.shape, 0)
    terms = [packet]
    for mask in step_masks(group):
        first = 0 if mask >> inner_bits << inner_bits == mask else INNER_ROWS
        stop = packet.shape[0] if mask >> inner_bits == 0 else EDGE
        terms.append(jnp.where((row >= first) & (row < stop), swap(packet, mask), 0.0))
    while len(terms) > 1:
        terms = [terms[at] + terms[at + 1] for at in range(0, len(terms), 2)]
    return terms[0]


def merged(parts):
    whole = Scatter(None, jnp.concatenate([part.kept for part in parts], axis=2), parts[0].steps)
    whole.sent = tuple(
        jnp.concatenate(pieces, axis=2) for pieces in zip(*[part.sent for part in parts])
    )
    whole.at = parts[0].at
    return whole


def shards(
    latents,
    targets,
    horizon,
    memory_valid,
    embed,
    qkv_weight,
    out_weight,
    up_weight,
    down_weight,
    head_weight,
    gains,
    embed_rows,
    embed_cols,
    qkv_rows,
    qkv_cols,
    out_rows,
    out_cols,
    up_rows,
    up_cols,
    down_rows,
    down_cols,
    head_rows,
    head_cols,
    gain_second,
):
    samples = latents.shape[0]
    sizes = (lax.axis_size("dp"), lax.axis_size("fsdp"))
    highest = (sizes[0] * sizes[1]).bit_length() - 1
    gather_steps = [(bit,) for bit in reversed(range(3, highest))] + [(2, 1), (0,)]
    scatter_steps = gather_steps[::-1]
    mesh_plan = (sizes[0], sizes[1], gather_steps)
    core = (lax.axis_index("fsdp") & 1).astype(jnp.int32).reshape(1)

    out_turned = jnp.swapaxes(out_weight, 1, 2)
    down_turned = jnp.swapaxes(down_weight, 1, 2)
    masters = [qkv_weight, out_turned, up_weight, down_turned, embed.T, head_weight]
    widths = [qkv_weight.shape[2], out_weight.shape[2], up_weight.shape[2], down_weight.shape[1]]
    widths = widths + [embed.shape[0], head_weight.shape[1]]
    att_widths, ffn_widths = widths[0:2], widths[2:4]
    chunk_widths = [
        att_widths + widths[4:5],
        ffn_widths + att_widths,
        ffn_widths + att_widths + ffn_widths + widths[5:6],
    ]
    chunks = [Gather(piece, gather_steps) for piece in run_pack(masters, chunk_widths)]
    first, second, third = chunks
    latent_rows = latents.transpose(0, 2, 1)
    target_rows = targets.transpose(0, 2, 1)
    shared = (gains, memory_valid, core)
    back_shared = (gains, core)

    count = len(gather_steps)
    flat = lambda item: item if item.ndim == 2 else item.reshape(1, -1)
    inner = [flat(item) for item in (qkv_rows, out_rows, up_rows, down_cols, embed_cols, head_rows)]
    outer = [flat(item) for item in (qkv_cols, out_cols, up_cols, down_rows, embed_rows, head_cols)]
    row_stats = [inner[at] if ROW_IS_INNER[at] else outer[at] for at in range(6)]
    first_row = run_first(masters, row_stats)
    for at in range(count - 1):
        for chunk in chunks:
            chunk.send()
        if at == 0:
            first.others, first_row = tie(first.others, first_row)
        for chunk in chunks[: 2 if at == count - 2 else 3]:
            chunk.join()
            if at == count - 3 and chunk is first:
                first.held, third.held = tie(first.held, third.held)
    first.send()
    (other,) = first.others
    held, other, second.held = tie(first.held, other, second.held)
    second.send()
    kept = [run_forward(0, chunk_widths[0], mesh_plan, latent_rows, held, other, *shared)]
    middle, (other,) = tie(kept[0][1], second.others)
    kept.append(
        run_forward(1, chunk_widths[1], mesh_plan, middle, second.held, other, *shared)
    )
    middle, third.others = tie(kept[1][1], third.others)
    third.join()
    third.send()
    (other,) = third.others
    dmiddle, sent, held, gain_middle, loss, counted = run_middle(
        chunk_widths[2],
        mesh_plan,
        middle,
        third.held,
        other,
        target_rows,
        gains,
        memory_valid,
        horizon,
        core,
    )
    pair = Scatter(sent, held, scatter_steps)
    pair.send()
    pair.join()
    like = first.held
    before = (kept[0][1], kept[1][6], kept[1][8], kept[1][7])
    dmiddle, pair.sent = tie(dmiddle, pair.sent)
    pair.send()
    dmiddle, sent, held, gain_one = run_backward(
        1, chunk_widths[1], mesh_plan, like, kept[1], dmiddle, *back_shared, before
    )
    dmiddle, sent, held, pair.others = tie(dmiddle, sent, held, pair.others)
    one = Scatter(sent, held, scatter_steps)
    one.send()
    pair.join()
    one.join()
    dmiddle, pair.sent, one.sent = tie(dmiddle, pair.sent, one.sent)
    one.send()
    pair.send()
    sent, held, gain_zero = run_backward(
        0, chunk_widths[0], mesh_plan, like, kept[0], dmiddle, *back_shared, latent_rows
    )
    sent, held, pair.others, one.others = tie(sent, held, pair.others, one.others)
    zero = Scatter(sent, held, scatter_steps)
    zero.send()
    one.join()
    one.send()
    pair.join()
    zero.join()
    one.others = behind(one.others, zero.sent)
    zero.send()
    one.join()
    early = merged([pair, one])
    while early.at < count:
        early.send()
        if early.at == count - 1:
            zero.join()
            zero.send()
        zero.others, early.others = tie(zero.others, early.others)
        early.join()
    raw_early = early.kept[0]

    packet = run_early(
        widths, raw_early, first_row, [gain_middle, gain_one], loss, counted
    )
    while zero.at < count:
        zero.join()
        if zero.at < count:
            zero.send()
    raw_late = zero.kept[0]
    packet = run_late(widths, packet, raw_late, gain_zero)
    inner_bits = sizes[1].bit_length() - 1
    rest = list(range(3, highest))
    groups = [(0,), (2, 1)] + [tuple(rest[at : at + 2][::-1]) for at in range(0, len(rest), 2)]
    for group in groups:
        packet = sum_packets(packet, group, inner_bits)
    results = run_update(
        widths, sizes, packet, raw_early, raw_late, masters, inner, outer, gains, gain_second
    )
    results = list(results)
    for at in range(3):
        results[at] = results[at].reshape(())
    for at in (3, 4, 11, 12, 19, 20):
        results[at] = jnp.swapaxes(results[at], -1, -2)
    for at in (5, 6, 25, 26):
        results[at] = results[at].reshape(-1)
    return tuple(results)


def solution(mesh):
    return jax.shard_map(
        shards,
        mesh=mesh,
        in_specs=(
            P(("dp", "fsdp"), None, None),
            P(("dp", "fsdp"), None, None),
            P(("dp", "fsdp")),
            P(("dp", "fsdp")),
            P("dp", "fsdp"),
            P(None, "fsdp", "dp"),
            P(None, "fsdp", "dp"),
            P(None, "fsdp", "dp"),
            P(None, "dp", "fsdp"),
            P("fsdp", "dp"),
            P(),
            P("dp"),
            P("fsdp"),
            P(None, "fsdp"),
            P(None, "dp"),
            P(None, "fsdp"),
            P(None, "dp"),
            P(None, "fsdp"),
            P(None, "dp"),
            P(None, "dp"),
            P(None, "fsdp"),
            P("fsdp"),
            P("dp"),
            P(),
        ),
        out_specs=(
            P(),
            P(),
            P(),
            P("dp", "fsdp"),
            P("dp", "fsdp"),
            P("dp"),
            P("fsdp"),
            P(None, "fsdp", "dp"),
            P(None, "fsdp", "dp"),
            P(None, "fsdp"),
            P(None, "dp"),
            P(None, "fsdp", "dp"),
            P(None, "fsdp", "dp"),
            P(None, "fsdp"),
            P(None, "dp"),
            P(None, "fsdp", "dp"),
            P(None, "fsdp", "dp"),
            P(None, "fsdp"),
            P(None, "dp"),
            P(None, "dp", "fsdp"),
            P(None, "dp", "fsdp"),
            P(None, "dp"),
            P(None, "fsdp"),
            P("fsdp", "dp"),
            P("fsdp", "dp"),
            P("fsdp"),
            P("dp"),
            P(),
            P(),
            P(),
        ),
        check_vma=False,
    )
```

profile of v0, /device:TPU:0, one launch (start us, length us, event | category | flops | bytes accessed | tf_op | source)
XLA Modules:
  0.0 191.7 jit_solution(7067107952559664190)
XLA Ops:
  0.7 1.8 pack.1
  2.5 4.0 %collective-permute-start = (bf16[1,64,256]{2,1,0:T(8,128)(2,1)}, bf16[1,64,256]{2,1,0:T(8,128)(2,1)S(1)}, u32[]{:S(2)}, u32[]{:S(2)}) collective-permute-start(bf16[1,64,256]{2,1,0:T(8,128)(2,1)} %bitcast.127), channel_id=1, source_target_pairs={{0,16},{1,17},{2,18},{3,19},{4,20},{5,21},{6,22},{7,23},{8,24},{9,... | collective-permute-start | bytes 98312 | tf_op jit(solution)/shard_map/ppermute | solution.py:1101
  6.6 2.9 %collective-permute-start.2 = (bf16[1,64,768]{2,1,0:T(8,128)(2,1)}, bf16[1,64,768]{2,1,0:T(8,128)(2,1)S(1)}, u32[]{:S(2)}, u32[]{:S(2)}) collective-permute-start(bf16[1,64,768]{2,1,0:T(8,128)(2,1)} %bitcast.125), channel_id=1, source_target_pairs={{0,16},{1,17},{2,18},{3,19},{4,20},{5,21},{6,22},{7,23},{8,24},{9,... | collective-permute-start | bytes 294920 | tf_op jit(solution)/shard_map/ppermute | solution.py:1101
  9.5 1.8 first_statistics.1.refs_1_
  12.1 1.6 collective-permute-start.1
  13.7 1.6 collective-permute-done.7
  16.2 1.7 collective-permute-done.1
  18.0 2.5 %collective-permute-start.3 = (bf16[4,64,256]{2,1,0:T(8,128)(2,1)S(1)}, bf16[4,64,256]{2,1,0:T(8,128)(2,1)S(1)}, u32[]{:S(2)}, u32[]{:S(2)}) collective-permute-start(bf16[4,64,256]{2,1,0:T(8,128)(2,1)S(1)} %pad_maximum_fusion.7), channel_id=1, source_target_pairs={{0,6},{1,7},{2,4},{3,5},{4,2},{5,3},{6,0},{7,1},{8,14},{9,15},{10,... | collective-permute-start | bytes 393224 | tf_op jit(solution)/shard_map/ppermute | solution.py:1101
  21.6 1.6 collective-permute-start.10
  23.2 1.5 collective-permute-start.11
  25.4 2.4 %collective-permute-start.9 = (bf16[4,64,384]{2,1,0:T(8,128)(2,1)S(1)}, bf16[4,64,384]{2,1,0:T(8,128)(2,1)S(1)}, u32[]{:S(2)}, u32[]{:S(2)}) collective-permute-start(bf16[4,64,384]{2,1,0:T(8,128)(2,1)S(1)} %pad_maximum_fusion.5), channel_id=1, source_target_pairs={{0,6},{1,7},{2,4},{3,5},{4,2},{5,3},{6,0},{7,1},{8,14},{9,15},{10,... | collective-permute-start | bytes 589832 | tf_op jit(solution)/shard_map/ppermute | solution.py:1101
  29.1 3.4 %collective-permute-done.10 = bf16[4,64,384]{2,1,0:T(8,128)(2,1)S(1)} collective-permute-done((bf16[4,64,384]{2,1,0:T(8,128)(2,1)S(1)}, bf16[4,64,384]{2,1,0:T(8,128)(2,1)S(1)}, u32[]{:S(2)}, u32[]{:S(2)}) %collective-permute-start.10) | collective-permute-done | bytes 196640 | tf_op jit(solution)/shard_map/ppermute | solution.py:1101
  32.5 2.3 %collective-permute-done.11 = bf16[4,64,384]{2,1,0:T(8,128)(2,1)S(1)} collective-permute-done((bf16[4,64,384]{2,1,0:T(8,128)(2,1)S(1)}, bf16[4,64,384]{2,1,0:T(8,128)(2,1)S(1)}, u32[]{:S(2)}, u32[]{:S(2)}) %collective-permute-start.11) | collective-permute-done | bytes 196640 | tf_op jit(solution)/shard_map/ppermute | solution.py:1101
  37.7 1.5 collective-permute-start.15
  39.2 1.3 collective-permute-start.16
  40.6 10.2 %forward_part.2 = (f32[1536,256]{1,0:T(8,128)}, f32[1536,256]{1,0:T(8,128)}, bf16[1536,768]{1,0:T(8,128)(2,1)}, bf16[1536,256]{1,0:T(8,128)(2,1)}, bf16[16,2,96,...) custom-call(s32[16,32,96]{2,1,0:T(8,128)S(1)} %bitcast.104, bf16[16,64,256]{2,1,0:T(8,128)(2,1)S(1)} %pad_maximum_fusion.2.own_ref, ...), custom_call_target="tpu_custom_call" | custom-call | flops 2415919104 | bytes 9437184 | tf_op jit(solution)/shard_map/forward_part/pallas_call | solution.py:378
  50.8 14.3 %forward_part.3 = (f32[1536,256]{1,0:T(8,128)}, f32[1536,256]{1,0:T(8,128)}, bf16[1536,768]{1,0:T(8,128)(2,1)}, bf16[1536,256]{1,0:T(8,128)(2,1)}, bf16[16,2,96,...) custom-call(f32[1536,256]{1,0:T(8,128)} %get-tuple-element.137.sourc, ...), custom_call_target="tpu_custom_call" | custom-call | flops 2415919104 | bytes 9437184 | tf_op jit(solution)/shard_map/forward_part/pallas_call | solution.py:378
  65.6 3.4 %collective-permute-done.17.refs_2_ = bf16[16,64,768]{2,1,0:T(8,128)(2,1)S(1)} collective-permute-done((bf16[16,64,768]{2,1,0:T(8,128)(2,1)S(1)}, bf16[16,64,768]{2,1,0:T(8,128)(2,1)S(1)}, u32[]{:S(2)}, u32[]{:S(2)}) %collective-permute-start.17) | collective-permute-done | bytes 1572896 | tf_op jit(solution)/shard_map/ppermute | solution.py:1101
  69.0 28.0 %middle_part.1 = (f32[1536,256]{1,0:T(8,128)}, bf16[16,64,768]{2,1,0:T(8,128)(2,1)S(1)}, bf16[16,64,768]{2,1,0:T(8,128)(2,1)S(1)}, f32[4,256]{1,0:T(4,128)}, f32[1,1]{1,0:T(1,128)}, /*index=5*/f32[1,1]{1,0:T(1,128)}) custom-call(f32[1536,256]{1,0:T(8,128)S(1)} %copy-done.5, bf16[16,64,768]{2,1,0:T(8,128)(2,1)S(1)} %pad_maximum_fusion.refs_1_, ...), custom_call_target="tpu_custom_call" | custom-call | flops 19327352832 | bytes 18874368 | tf_op jit(solution)/shard_map/middle_part/pallas_call | solution.py:610
  97.1 3.4 %collective-permute-done.18 = bf16[16,64,768]{2,1,0:T(8,128)(2,1)} collective-permute-done((bf16[16,64,768]{2,1,0:T(8,128)(2,1)S(1)}, bf16[16,64,768]{2,1,0:T(8,128)(2,1)}, u32[]{:S(2)}, u32[]{:S(2)}) %collective-permute-start.18) | collective-permute-done | bytes 1572896 | tf_op jit(solution)/shard_map/ppermute | solution.py:1101
  100.5 1.7 convert_add_fusion
  103.0 1.5 collective-permute-start.20
  104.5 1.3 collective-permute-start.21
  105.8 16.6 %backward_part.2 = (f32[1536,256]{1,0:T(8,128)}, bf16[16,64,384]{2,1,0:T(8,128)(2,1)S(1)}, bf16[16,64,384]{2,1,0:T(8,128)(2,1)S(1)}, f32[2,256]{1,0:T(2,128)}) custom-call(f32[1536,256]{1,0:T(8,128)} %get-tuple-element.147.refs_0_, bf16[1536,768]{1,0:T(8,128)(2,1)} %get-tuple-element.148.refs_1_, bf16[1536,256]{1,0:T(8,128)(2,1)} %get-tuple-element.149.refs_2_, ...), custom_call_target="tpu_custom_call" | custom-call | flops 7247757312 | bytes 14155776 | tf_op jit(solution)/shard_map/backward_part/pallas_call | solution.py:772
  123.2 1.4 convert_add_fusion.2
  125.6 1.4 fusion.7
  127.6 1.2 collective-permute-start.24
  128.8 1.6 collective-permute-start.25
  131.1 12.5 %backward_part.3 = (bf16[16,64,256]{2,1,0:T(8,128)(2,1)S(1)}, bf16[16,64,256]{2,1,0:T(8,128)(2,1)S(1)}, f32[2,256]{1,0:T(2,128)}) custom-call(f32[1536,256]{1,0:T(8,128)} %get-tuple-element.166.refs_0_, bf16[1536,768]{1,0:T(8,128)(2,1)} %get-tuple-element.167.refs_1_, bf16[1536,256]{1,0:T(8,128)(2,1)} %get-tuple-element.168.refs_2_, ...), custom_call_target="tpu_custom_call" | custom-call | flops 4831838208 | bytes 12582912 | tf_op jit(solution)/shard_map/backward_part/pallas_call | solution.py:772
  144.4 1.2 fusion.12
  145.6 1.6 collective-permute-start.27
  148.1 1.5 collective-permute-start.30
  149.6 1.3 collective-permute-start.31
  151.0 2.5 %collective-permute-start.33 = (bf16[1,64,1152]{2,1,0:T(8,128)(2,1)S(1)}, bf16[1,64,1152]{2,1,0:T(8,128)(2,1)S(1)}, u32[]{:S(2)}, u32[]{:S(2)}) collective-permute-start(bf16[1,64,1152]{2,1,0:T(8,128)(2,1)S(1)} %pad_maximum_fusion.6), channel_id=1, source_target_pairs={{0,16},{1,17},{2,18},{3,19},{4,20},{5,21},{6,22},{7,23},{8,24},{9,... | collective-permute-start | bytes 442376 | tf_op jit(solution)/shard_map/ppermute | solution.py:1101
  154.3 2.8 %collective-permute-done.31 = bf16[4,64,256]{2,1,0:T(8,128)(2,1)S(1)} collective-permute-done((bf16[4,64,256]{2,1,0:T(8,128)(2,1)S(1)}, bf16[4,64,256]{2,1,0:T(8,128)(2,1)S(1)}, u32[]{:S(2)}, u32[]{:S(2)}) %collective-permute-start.31) | collective-permute-done | bytes 131104 | tf_op jit(solution)/shard_map/ppermute | solution.py:1101
  157.8 2.9 %collective-permute-done.33 = bf16[1,64,1152]{2,1,0:T(8,128)(2,1)S(1)} collective-permute-done((bf16[1,64,1152]{2,1,0:T(8,128)(2,1)S(1)}, bf16[1,64,1152]{2,1,0:T(8,128)(2,1)S(1)}, u32[]{:S(2)}, u32[]{:S(2)}) %collective-permute-start.33) | collective-permute-done | bytes 147488 | tf_op jit(solution)/shard_map/ppermute | solution.py:1101
  160.7 1.3 collective-permute-done.32
  163.7 3.2 %early_statistics.1.early_ref = f32[48,128]{1,0:T(8,128)} custom-call(f32[64,1152]{1,0:T(8,128)} %fusion.3.refs_0_.refs_1_, f32[1,128]{1,0:T(1,128)} %first_statistics.1.refs_1_, f32[4,256]{1,0:T(4,128)} %get-tuple-element.190.refs_2_, f32[2,256]{1,0:T(2,128)} %get-tuple-element.191.refs_3_, f32[1,1]{1,0:T(1,128)} %get-tuple-element.192.refs_4_, ...), custom_call_target="tpu_custom_call" | custom-call | tf_op jit(solution)/shard_map/early_statistics/pallas_call | solution.py:971
  167.6 1.7 late_statistics.1
  169.3 1.4 collective-permute-done.35
  171.5 1.1 collective-permute-start.36
  172.6 1.6 collective-permute-start.37
  176.4 2.5 %collective-permute-done.38 = f32[48,128]{1,0:T(8,128)S(1)} collective-permute-done((f32[48,128]{1,0:T(8,128)S(1)}, f32[48,128]{1,0:T(8,128)S(1)}, u32[]{:S(2)}, u32[]{:S(2)}) %collective-permute-start.38) | collective-permute-done | bytes 24608 | tf_op jit(solution)/shard_map/ppermute | solution.py:1101
  179.0 1.8 collective-permute-start.39
  181.7 1.7 collective-permute-start.41
  183.4 2.1 %collective-permute-done.40 = f32[48,128]{1,0:T(8,128)S(1)} collective-permute-done((f32[48,128]{1,0:T(8,128)S(1)}, f32[48,128]{1,0:T(8,128)S(1)}, u32[]{:S(2)}, u32[]{:S(2)}) %collective-permute-start.40) | collective-permute-done | bytes 24608 | tf_op jit(solution)/shard_map/ppermute | solution.py:1101
  185.6 1.8 collective-permute-done.41
  188.0 3.5 %update.1 = (f32[1,1]{1,0:T(1,128)}, f32[1,1]{1,0:T(1,128)}, f32[1,1]{1,0:T(1,128)}, f32[64,128]{1,0:T(8,128)}, f32[64,128]{1,0:T(8,128)}, /*index=5*/f32[1,128]...) custom-call(f32[48,128]{1,0:T(8,128)} %add_add_fusion.refs_0_, ...), custom_call_target="tpu_custom_call" | custom-call | tf_op jit(solution)/shard_map/update/pallas_call | solution.py:1090
  (101 shorter events, 22.2 us)
Async XLA Ops:
  2.5 15.4 %copy-start.9 = (bf16[64,768]{1,0:T(8,128)(2,1)S(1)}, bf16[64,768]{1,0:T(8,128)(2,1)}, u32[]{:S(2)}) copy-start(bf16[64,768]{1,0:T(8,128)(2,1)} %get-tuple-element.130) | copy-start | bytes 294916
  2.5 8.8 %collective-permute-start = (bf16[1,64,256]{2,1,0:T(8,128)(2,1)}, bf16[1,64,256]{2,1,0:T(8,128)(2,1)S(1)}, u32[]{:S(2)}, u32[]{:S(2)}) collective-permute-start(bf16[1,64,256]{2,1,0:T(8,128)(2,1)} %bitcast.127), channel_id=1, source_target_pairs={{0,16},{1,17},{2,18},{3,19},{4,20},{5,21},{6,22},{7,23},{8,24},{9,... | collective-permute-start | bytes 98312 | tf_op jit(solution)/shard_map/ppermute | solution.py:1101
  6.6 8.7 %collective-permute-start.7 = (bf16[1,64,384]{2,1,0:T(8,128)(2,1)}, bf16[1,64,384]{2,1,0:T(8,128)(2,1)S(1)}, u32[]{:S(2)}, u32[]{:S(2)}) collective-permute-start(bf16[1,64,384]{2,1,0:T(8,128)(2,1)} %bitcast.126), channel_id=1, source_target_pairs={{0,16},{1,17},{2,18},{3,19},{4,20},{5,21},{6,22},{7,23},{8,24},{9,... | collective-permute-start | bytes 147464 | tf_op jit(solution)/shard_map/ppermute | solution.py:1101
  6.6 11.3 %collective-permute-start.2 = (bf16[1,64,768]{2,1,0:T(8,128)(2,1)}, bf16[1,64,768]{2,1,0:T(8,128)(2,1)S(1)}, u32[]{:S(2)}, u32[]{:S(2)}) collective-permute-start(bf16[1,64,768]{2,1,0:T(8,128)(2,1)} %bitcast.125), channel_id=1, source_target_pairs={{0,16},{1,17},{2,18},{3,19},{4,20},{5,21},{6,22},{7,23},{8,24},{9,... | collective-permute-start | bytes 294920 | tf_op jit(solution)/shard_map/ppermute | solution.py:1101
  12.1 5.8 %collective-permute-start.1 = (bf16[2,64,256]{2,1,0:T(8,128)(2,1)S(1)}, bf16[2,64,256]{2,1,0:T(8,128)(2,1)S(1)}, u32[]{:S(2)}, u32[]{:S(2)}) collective-permute-start(bf16[2,64,256]{2,1,0:T(8,128)(2,1)S(1)} %pad_maximum_fusion.9), channel_id=1, source_target_pairs={{0,8},{1,9},{2,10},{3,11},{4,12},{5,13},{6,14},{7,15},{8,0},{9,1},... | collective-permute-start | bytes 196616 | tf_op jit(solution)/shard_map/ppermute | solution.py:1101
  16.1 5.4 %collective-permute-start.8 = (bf16[2,64,384]{2,1,0:T(8,128)(2,1)S(1)}, bf16[2,64,384]{2,1,0:T(8,128)(2,1)S(1)}, u32[]{:S(2)}, u32[]{:S(2)}) collective-permute-start(bf16[2,64,384]{2,1,0:T(8,128)(2,1)S(1)} %pad_maximum_fusion.8), channel_id=1, source_target_pairs={{0,8},{1,9},{2,10},{3,11},{4,12},{5,13},{6,14},{7,15},{8,0},{9,1},... | collective-permute-start | bytes 294920 | tf_op jit(solution)/shard_map/ppermute | solution.py:1101
  18.0 17.1 %copy-start.6 = (bf16[2,64,768]{2,1,0:T(8,128)(2,1)}, bf16[2,64,768]{2,1,0:T(8,128)(2,1)S(1)}, u32[]{:S(2)}) copy-start(bf16[2,64,768]{2,1,0:T(8,128)(2,1)S(1)} %pad_maximum_fusion.4) | copy-start | bytes 589828
  18.0 7.4 %collective-permute-start.3 = (bf16[4,64,256]{2,1,0:T(8,128)(2,1)S(1)}, bf16[4,64,256]{2,1,0:T(8,128)(2,1)S(1)}, u32[]{:S(2)}, u32[]{:S(2)}) collective-permute-start(bf16[4,64,256]{2,1,0:T(8,128)(2,1)S(1)} %pad_maximum_fusion.7), channel_id=1, source_target_pairs={{0,6},{1,7},{2,4},{3,5},{4,2},{5,3},{6,0},{7,1},{8,14},{9,15},{10,... | collective-permute-start | bytes 393224 | tf_op jit(solution)/shard_map/ppermute | solution.py:1101
  20.5 7.8 %collective-permute-start.4 = (bf16[4,64,256]{2,1,0:T(8,128)(2,1)S(1)}, bf16[4,64,256]{2,1,0:T(8,128)(2,1)S(1)}, u32[]{:S(2)}, u32[]{:S(2)}) collective-permute-start(bf16[4,64,256]{2,1,0:T(8,128)(2,1)S(1)} %pad_maximum_fusion.7), channel_id=1, source_target_pairs={{0,4},{1,5},{2,6},{3,7},{4,0},{5,1},{6,2},{7,3},{8,12},{9,13},{10,... | collective-permute-start | bytes 393224 | tf_op jit(solution)/shard_map/ppermute | solution.py:1101
  21.1 7.2 %collective-permute-start.5 = (bf16[4,64,256]{2,1,0:T(8,128)(2,1)S(1)}, bf16[4,64,256]{2,1,0:T(8,128)(2,1)S(1)}, u32[]{:S(2)}, u32[]{:S(2)}) collective-permute-start(bf16[4,64,256]{2,1,0:T(8,128)(2,1)S(1)} %pad_maximum_fusion.7), channel_id=1, source_target_pairs={{0,2},{1,3},{2,0},{3,1},{4,6},{5,7},{6,4},{7,5},{8,10},{9,11},{10,... | collective-permute-start | bytes 393224 | tf_op jit(solution)/shard_map/ppermute | solution.py:1101
  21.6 10.9 %collective-permute-start.10 = (bf16[4,64,384]{2,1,0:T(8,128)(2,1)S(1)}, bf16[4,64,384]{2,1,0:T(8,128)(2,1)S(1)}, u32[]{:S(2)}, u32[]{:S(2)}) collective-permute-start(bf16[4,64,384]{2,1,0:T(8,128)(2,1)S(1)} %pad_maximum_fusion.5), channel_id=1, source_target_pairs={{0,4},{1,5},{2,6},{3,7},{4,0},{5,1},{6,2},{7,3},{8,12},{9,13},{10,... | collective-permute-start | bytes 589832 | tf_op jit(solution)/shard_map/ppermute | solution.py:1101
  23.2 11.6 %collective-permute-start.11 = (bf16[4,64,384]{2,1,0:T(8,128)(2,1)S(1)}, bf16[4,64,384]{2,1,0:T(8,128)(2,1)S(1)}, u32[]{:S(2)}, u32[]{:S(2)}) collective-permute-start(bf16[4,64,384]{2,1,0:T(8,128)(2,1)S(1)} %pad_maximum_fusion.5), channel_id=1, source_target_pairs={{0,2},{1,3},{2,0},{3,1},{4,6},{5,7},{6,4},{7,5},{8,10},{9,11},{10,... | collective-permute-start | bytes 589832 | tf_op jit(solution)/shard_map/ppermute | solution.py:1101
  25.4 9.3 %collective-permute-start.9 = (bf16[4,64,384]{2,1,0:T(8,128)(2,1)S(1)}, bf16[4,64,384]{2,1,0:T(8,128)(2,1)S(1)}, u32[]{:S(2)}, u32[]{:S(2)}) collective-permute-start(bf16[4,64,384]{2,1,0:T(8,128)(2,1)S(1)} %pad_maximum_fusion.5), channel_id=1, source_target_pairs={{0,6},{1,7},{2,4},{3,5},{4,2},{5,3},{6,0},{7,1},{8,14},{9,15},{10,... | collective-permute-start | bytes 589832 | tf_op jit(solution)/shard_map/ppermute | solution.py:1101
  28.4 6.6 %collective-permute-start.6 = (bf16[16,64,256]{2,1,0:T(8,128)(2,1)S(1)}, bf16[16,64,256]{2,1,0:T(8,128)(2,1)S(1)}, u32[]{:S(2)}, u32[]{:S(2)}) collective-permute-start(bf16[16,64,256]{2,1,0:T(8,128)(2,1)S(1)} %pad_maximum_fusion.2.own_ref), channel_id=1, source_target_pairs={{0,1},{1,0},{2,3},{3,2},{4,5},{5,4},{6,7},{7,6},{8,9},{9,8},{10,11... | collective-permute-start | bytes 1572872 | tf_op jit(solution)/shard_map/ppermute | solution.py:1101
  28.5 7.4 %collective-permute-start.13 = (bf16[2,64,768]{2,1,0:T(8,128)(2,1)S(1)}, bf16[2,64,768]{2,1,0:T(8,128)(2,1)}, u32[]{:S(2)}, u32[]{:S(2)}) collective-permute-start(bf16[2,64,768]{2,1,0:T(8,128)(2,1)S(1)} %pad_maximum_fusion.4), channel_id=1, source_target_pairs={{0,8},{1,9},{2,10},{3,11},{4,12},{5,13},{6,14},{7,15},{8,0},{9,1},... | collective-permute-start | bytes 589832 | tf_op jit(solution)/shard_map/ppermute | solution.py:1101
  34.9 5.7 %copy-start = (f32[7,256]{1,0:T(8,128)S(1)}, f32[7,256]{1,0:T(8,128)}, u32[]{:S(2)}) copy-start(f32[7,256]{1,0:T(8,128)} %refs_21_.1) | copy-start | bytes 21508
  34.9 5.7 %copy-start.2 = (s32[16,96,32]{1,2,0:T(8,128)S(1)}, s32[16,96,32]{1,2,0:T(8,128)}, u32[]{:S(2)}) copy-start(s32[16,96,32]{1,2,0:T(8,128)} %param.24) | copy-start | bytes 589828
  34.9 5.7 %copy-start.3 = (s32[16]{0:T(128)S(1)}, s32[16]{0:T(128)}, u32[]{:S(2)}) copy-start(s32[16]{0:T(128)} %refs_5_.6) | copy-start | bytes 196
  35.1 15.7 %collective-permute-start.12 = (bf16[16,64,384]{2,1,0:T(8,128)(2,1)S(1)}, bf16[16,64,384]{2,1,0:T(8,128)(2,1)S(1)}, u32[]{:S(2)}, u32[]{:S(2)}) collective-permute-start(bf16[16,64,384]{2,1,0:T(8,128)(2,1)S(1)} %pad_maximum_fusion.1.own_ref), channel_id=1, source_target_pairs={{0,1},{1,0},{2,3},{3,2},{4,5},{5,4},{6,7},{7,6},{8,9},{9,8},{10,11... | collective-permute-start | bytes 2359304 | tf_op jit(solution)/shard_map/ppermute | solution.py:1101
  37.0 28.1 %collective-permute-start.14 = (bf16[4,64,768]{2,1,0:T(8,128)(2,1)S(1)}, bf16[4,64,768]{2,1,0:T(8,128)(2,1)S(1)}, u32[]{:S(2)}, u32[]{:S(2)}) collective-permute-start(bf16[4,64,768]{2,1,0:T(8,128)(2,1)S(1)} %pad_maximum_fusion.3), channel_id=1, source_target_pairs={{0,2},{1,3},{2,0},{3,1},{4,6},{5,7},{6,4},{7,5},{8,10},{9,11},{10,... | collective-permute-start | bytes 1179656 | tf_op jit(solution)/shard_map/ppermute | solution.py:1101
  37.7 27.4 %collective-permute-start.15 = (bf16[4,64,768]{2,1,0:T(8,128)(2,1)S(1)}, bf16[4,64,768]{2,1,0:T(8,128)(2,1)S(1)}, u32[]{:S(2)}, u32[]{:S(2)}) collective-permute-start(bf16[4,64,768]{2,1,0:T(8,128)(2,1)S(1)} %pad_maximum_fusion.3), channel_id=1, source_target_pairs={{0,4},{1,5},{2,6},{3,7},{4,0},{5,1},{6,2},{7,3},{8,12},{9,13},{10,... | collective-permute-start | bytes 1179656 | tf_op jit(solution)/shard_map/ppermute | solution.py:1101
  39.2 25.9 %collective-permute-start.16 = (bf16[4,64,768]{2,1,0:T(8,128)(2,1)S(1)}, bf16[4,64,768]{2,1,0:T(8,128)(2,1)S(1)}, u32[]{:S(2)}, u32[]{:S(2)}) collective-permute-start(bf16[4,64,768]{2,1,0:T(8,128)(2,1)S(1)} %pad_maximum_fusion.3), channel_id=1, source_target_pairs={{0,6},{1,7},{2,4},{3,5},{4,2},{5,3},{6,0},{7,1},{8,14},{9,15},{10,... | collective-permute-start | bytes 1179656 | tf_op jit(solution)/shard_map/ppermute | solution.py:1101
  65.3 3.7 %copy-start.1 = (s32[16,48,32]{1,2,0:T(8,128)S(1)}, s32[16,48,32]{1,2,0:T(8,128)}, u32[]{:S(2)}) copy-start(s32[16,48,32]{1,2,0:T(8,128)} %param.25) | copy-start | bytes 294916
  65.5 3.5 %collective-permute-start.17 = (bf16[16,64,768]{2,1,0:T(8,128)(2,1)S(1)}, bf16[16,64,768]{2,1,0:T(8,128)(2,1)S(1)}, u32[]{:S(2)}, u32[]{:S(2)}) collective-permute-start(bf16[16,64,768]{2,1,0:T(8,128)(2,1)S(1)} %pad_maximum_fusion.refs_1_), channel_id=1, source_target_pairs={{0,1},{1,0},{2,3},{3,2},{4,5},{5,4},{6,7},{7,6},{8,9},{9,8},{10,11... | collective-permute-start | bytes 4718600 | tf_op jit(solution)/shard_map/ppermute | solution.py:1101
  97.0 3.5 %collective-permute-start.18 = (bf16[16,64,768]{2,1,0:T(8,128)(2,1)S(1)}, bf16[16,64,768]{2,1,0:T(8,128)(2,1)}, u32[]{:S(2)}, u32[]{:S(2)}) collective-permute-start(bf16[16,64,768]{2,1,0:T(8,128)(2,1)S(1)} %get-tuple-element.146), channel_id=1, source_target_pairs={{0,1},{1,0},{2,3},{3,2},{4,5},{5,4},{6,7},{7,6},{8,9},{9,8},{10,11... | collective-permute-start | bytes 4718600 | tf_op jit(solution)/shard_map/ppermute | solution.py:1101
  102.3 20.2 %collective-permute-start.19 = (bf16[4,64,768]{2,1,0:T(8,128)(2,1)S(1)}, bf16[4,64,768]{2,1,0:T(8,128)(2,1)S(1)}, u32[]{:S(2)}, u32[]{:S(2)}) collective-permute-start(bf16[4,64,768]{2,1,0:T(8,128)(2,1)S(1)} %get-tuple-element.160), channel_id=1, source_target_pairs={{0,2},{1,3},{2,0},{3,1},{4,6},{5,7},{6,4},{7,5},{8,10},{9,11},{10,... | collective-permute-start | bytes 1179656 | tf_op jit(solution)/shard_map/ppermute | solution.py:1101
  103.0 19.5 %collective-permute-start.20 = (bf16[4,64,768]{2,1,0:T(8,128)(2,1)S(1)}, bf16[4,64,768]{2,1,0:T(8,128)(2,1)}, u32[]{:S(2)}, u32[]{:S(2)}) collective-permute-start(bf16[4,64,768]{2,1,0:T(8,128)(2,1)S(1)} %get-tuple-element.161), channel_id=1, source_target_pairs={{0,4},{1,5},{2,6},{3,7},{4,0},{5,1},{6,2},{7,3},{8,12},{9,13},{10,... | collective-permute-start | bytes 1179656 | tf_op jit(solution)/shard_map/ppermute | solution.py:1101
  104.5 18.7 %collective-permute-start.21 = (bf16[4,64,768]{2,1,0:T(8,128)(2,1)S(1)}, bf16[4,64,768]{2,1,0:T(8,128)(2,1)}, u32[]{:S(2)}, u32[]{:S(2)}) collective-permute-start(bf16[4,64,768]{2,1,0:T(8,128)(2,1)S(1)} %get-tuple-element.162), channel_id=1, source_target_pairs={{0,6},{1,7},{2,4},{3,5},{4,2},{5,3},{6,0},{7,1},{8,14},{9,15},{10,... | collective-permute-start | bytes 1179656 | tf_op jit(solution)/shard_map/ppermute | solution.py:1101
  123.2 2.4 %collective-permute-start.22 = (bf16[16,64,384]{2,1,0:T(8,128)(2,1)S(1)}, bf16[16,64,384]{2,1,0:T(8,128)(2,1)}, u32[]{:S(2)}, u32[]{:S(2)}) collective-permute-start(bf16[16,64,384]{2,1,0:T(8,128)(2,1)S(1)} %get-tuple-element.172), channel_id=1, source_target_pairs={{0,1},{1,0},{2,3},{3,2},{4,5},{5,4},{6,7},{7,6},{8,9},{9,8},{10,11... | collective-permute-start | bytes 2359304 | tf_op jit(solution)/shard_map/ppermute | solution.py:1101
  127.0 16.6 %collective-permute-start.23 = (bf16[2,64,768]{2,1,0:T(8,128)(2,1)S(1)}, bf16[2,64,768]{2,1,0:T(8,128)(2,1)S(1)}, u32[]{:S(2)}, u32[]{:S(2)}) collective-permute-start(bf16[2,64,768]{2,1,0:T(8,128)(2,1)S(1)} %get-tuple-element.177), channel_id=1, source_target_pairs={{0,8},{1,9},{2,10},{3,11},{4,12},{5,13},{6,14},{7,15},{8,0},{9,1},... | collective-permute-start | bytes 589832 | tf_op jit(solution)/shard_map/ppermute | solution.py:1101
  127.6 16.0 %collective-permute-start.24 = (bf16[4,64,384]{2,1,0:T(8,128)(2,1)S(1)}, bf16[4,64,384]{2,1,0:T(8,128)(2,1)}, u32[]{:S(2)}, u32[]{:S(2)}) collective-permute-start(bf16[4,64,384]{2,1,0:T(8,128)(2,1)S(1)} %get-tuple-element.178), channel_id=1, source_target_pairs={{0,2},{1,3},{2,0},{3,1},{4,6},{5,7},{6,4},{7,5},{8,10},{9,11},{10,... | collective-permute-start | bytes 589832 | tf_op jit(solution)/shard_map/ppermute | solution.py:1101
  128.8 14.9 %collective-permute-start.25 = (bf16[4,64,384]{2,1,0:T(8,128)(2,1)S(1)}, bf16[4,64,384]{2,1,0:T(8,128)(2,1)S(1)}, u32[]{:S(2)}, u32[]{:S(2)}) collective-permute-start(bf16[4,64,384]{2,1,0:T(8,128)(2,1)S(1)} %get-tuple-element.179), channel_id=1, source_target_pairs={{0,4},{1,5},{2,6},{3,7},{4,0},{5,1},{6,2},{7,3},{8,12},{9,13},{10,... | collective-permute-start | bytes 589832 | tf_op jit(solution)/shard_map/ppermute | solution.py:1101
  130.4 13.3 %collective-permute-start.26 = (bf16[4,64,384]{2,1,0:T(8,128)(2,1)S(1)}, bf16[4,64,384]{2,1,0:T(8,128)(2,1)S(1)}, u32[]{:S(2)}, u32[]{:S(2)}) collective-permute-start(bf16[4,64,384]{2,1,0:T(8,128)(2,1)S(1)} %get-tuple-element.180), channel_id=1, source_target_pairs={{0,6},{1,7},{2,4},{3,5},{4,2},{5,3},{6,0},{7,1},{8,14},{9,15},{10,... | collective-permute-start | bytes 589832 | tf_op jit(solution)/shard_map/ppermute | solution.py:1101
  144.4 2.9 %collective-permute-start.28 = (bf16[16,64,256]{2,1,0:T(8,128)(2,1)S(1)}, bf16[16,64,256]{2,1,0:T(8,128)(2,1)S(1)}, u32[]{:S(2)}, u32[]{:S(2)}) collective-permute-start(bf16[16,64,256]{2,1,0:T(8,128)(2,1)S(1)} %get-tuple-element.186), channel_id=1, source_target_pairs={{0,1},{1,0},{2,3},{3,2},{4,5},{5,4},{6,7},{7,6},{8,9},{9,8},{10,11... | collective-permute-start | bytes 1572872 | tf_op jit(solution)/shard_map/ppermute | solution.py:1101
  145.6 5.3 %collective-permute-start.27 = (bf16[2,64,384]{2,1,0:T(8,128)(2,1)S(1)}, bf16[2,64,384]{2,1,0:T(8,128)(2,1)S(1)}, u32[]{:S(2)}, u32[]{:S(2)}) collective-permute-start(bf16[2,64,384]{2,1,0:T(8,128)(2,1)S(1)} %get-tuple-element.244), channel_id=1, source_target_pairs={{0,8},{1,9},{2,10},{3,11},{4,12},{5,13},{6,14},{7,15},{8,0},{9,1},... | collective-permute-start | bytes 294920 | tf_op jit(solution)/shard_map/ppermute | solution.py:1101
  147.4 6.1 %collective-permute-start.29 = (bf16[4,64,256]{2,1,0:T(8,128)(2,1)S(1)}, bf16[4,64,256]{2,1,0:T(8,128)(2,1)S(1)}, u32[]{:S(2)}, u32[]{:S(2)}) collective-permute-start(bf16[4,64,256]{2,1,0:T(8,128)(2,1)S(1)} %get-tuple-element.243), channel_id=1, source_target_pairs={{0,2},{1,3},{2,0},{3,1},{4,6},{5,7},{6,4},{7,5},{8,10},{9,11},{10,... | collective-permute-start | bytes 393224 | tf_op jit(solution)/shard_map/ppermute | solution.py:1101
  148.1 6.1 %collective-permute-start.30 = (bf16[4,64,256]{2,1,0:T(8,128)(2,1)S(1)}, bf16[4,64,256]{2,1,0:T(8,128)(2,1)S(1)}, u32[]{:S(2)}, u32[]{:S(2)}) collective-permute-start(bf16[4,64,256]{2,1,0:T(8,128)(2,1)S(1)} %get-tuple-element.242), channel_id=1, source_target_pairs={{0,4},{1,5},{2,6},{3,7},{4,0},{5,1},{6,2},{7,3},{8,12},{9,13},{10,... | collective-permute-start | bytes 393224 | tf_op jit(solution)/shard_map/ppermute | solution.py:1101
  149.6 7.5 %collective-permute-start.31 = (bf16[4,64,256]{2,1,0:T(8,128)(2,1)S(1)}, bf16[4,64,256]{2,1,0:T(8,128)(2,1)S(1)}, u32[]{:S(2)}, u32[]{:S(2)}) collective-permute-start(bf16[4,64,256]{2,1,0:T(8,128)(2,1)S(1)} %get-tuple-element.241), channel_id=1, source_target_pairs={{0,6},{1,7},{2,4},{3,5},{4,2},{5,3},{6,0},{7,1},{8,14},{9,15},{10,... | collective-permute-start | bytes 393224 | tf_op jit(solution)/shard_map/ppermute | solution.py:1101
  151.0 9.6 %collective-permute-start.33 = (bf16[1,64,1152]{2,1,0:T(8,128)(2,1)S(1)}, bf16[1,64,1152]{2,1,0:T(8,128)(2,1)S(1)}, u32[]{:S(2)}, u32[]{:S(2)}) collective-permute-start(bf16[1,64,1152]{2,1,0:T(8,128)(2,1)S(1)} %pad_maximum_fusion.6), channel_id=1, source_target_pairs={{0,16},{1,17},{2,18},{3,19},{4,20},{5,21},{6,22},{7,23},{8,24},{9,... | collective-permute-start | bytes 442376 | tf_op jit(solution)/shard_map/ppermute | solution.py:1101
  157.2 4.8 %collective-permute-start.32 = (bf16[2,64,256]{2,1,0:T(8,128)(2,1)S(1)}, bf16[2,64,256]{2,1,0:T(8,128)(2,1)S(1)}, u32[]{:S(2)}, u32[]{:S(2)}) collective-permute-start(bf16[2,64,256]{2,1,0:T(8,128)(2,1)S(1)} %get-tuple-element.251), channel_id=1, source_target_pairs={{0,8},{1,9},{2,10},{3,11},{4,12},{5,13},{6,14},{7,15},{8,0},{9,1},... | collective-permute-start | bytes 196616 | tf_op jit(solution)/shard_map/ppermute | solution.py:1101
  162.0 5.0 %collective-permute-start.34 = (bf16[1,64,256]{2,1,0:T(8,128)(2,1)S(1)}, bf16[1,64,256]{2,1,0:T(8,128)(2,1)S(1)}, u32[]{:S(2)}, u32[]{:S(2)}) collective-permute-start(bf16[1,64,256]{2,1,0:T(8,128)(2,1)S(1)} %fusion.15), channel_id=1, source_target_pairs={{0,16},{1,17},{2,18},{3,19},{4,20},{5,21},{6,22},{7,23},{8,24},{9,... | collective-permute-start | bytes 98312 | tf_op jit(solution)/shard_map/ppermute | solution.py:1101
  169.2 1.4 collective-permute-start.35
  171.5 3.8 %collective-permute-start.36 = (f32[48,128]{1,0:T(8,128)S(1)}, f32[48,128]{1,0:T(8,128)S(1)}, u32[]{:S(2)}, u32[]{:S(2)}) collective-permute-start(f32[48,128]{1,0:T(8,128)S(1)} %select_add_fusion), channel_id=1, source_target_pairs={{0,2},{1,3},{2,0},{3,1},{4,6},{5,7},{6,4},{7,5},{8,10},{9,11},{10,... | collective-permute-start | bytes 73736 | tf_op jit(solution)/shard_map/ppermute | solution.py:1101
  172.6 3.8 %collective-permute-start.37 = (f32[48,128]{1,0:T(8,128)S(1)}, f32[48,128]{1,0:T(8,128)S(1)}, u32[]{:S(2)}, u32[]{:S(2)}) collective-permute-start(f32[48,128]{1,0:T(8,128)S(1)} %select_add_fusion), channel_id=1, source_target_pairs={{0,4},{1,5},{2,6},{3,7},{4,0},{5,1},{6,2},{7,3},{8,12},{9,13},{10,... | collective-permute-start | bytes 73736 | tf_op jit(solution)/shard_map/ppermute | solution.py:1101
  174.2 4.7 %collective-permute-start.38 = (f32[48,128]{1,0:T(8,128)S(1)}, f32[48,128]{1,0:T(8,128)S(1)}, u32[]{:S(2)}, u32[]{:S(2)}) collective-permute-start(f32[48,128]{1,0:T(8,128)S(1)} %select_add_fusion), channel_id=1, source_target_pairs={{0,6},{1,7},{2,4},{3,5},{4,2},{5,3},{6,0},{7,1},{8,14},{9,15},{10,... | collective-permute-start | bytes 73736 | tf_op jit(solution)/shard_map/ppermute | solution.py:1101
  179.0 4.5 %collective-permute-start.39 = (f32[48,128]{1,0:T(8,128)S(1)}, f32[48,128]{1,0:T(8,128)S(1)}, u32[]{:S(2)}, u32[]{:S(2)}) collective-permute-start(f32[48,128]{1,0:T(8,128)S(1)} %add_add_fusion.1), channel_id=1, source_target_pairs={{0,8},{1,9},{2,10},{3,11},{4,12},{5,13},{6,14},{7,15},{8,0},{9,1},... | collective-permute-start | bytes 73736 | tf_op jit(solution)/shard_map/ppermute | solution.py:1101
  180.8 4.7 %collective-permute-start.40 = (f32[48,128]{1,0:T(8,128)S(1)}, f32[48,128]{1,0:T(8,128)S(1)}, u32[]{:S(2)}, u32[]{:S(2)}) collective-permute-start(f32[48,128]{1,0:T(8,128)S(1)} %add_add_fusion.1), channel_id=1, source_target_pairs={{0,16},{1,17},{2,18},{3,19},{4,20},{5,21},{6,22},{7,23},{8,24},{9,... | collective-permute-start | bytes 73736 | tf_op jit(solution)/shard_map/ppermute | solution.py:1101
  181.7 5.6 %collective-permute-start.41 = (f32[48,128]{1,0:T(8,128)S(1)}, f32[48,128]{1,0:T(8,128)S(1)}, u32[]{:S(2)}, u32[]{:S(2)}) collective-permute-start(f32[48,128]{1,0:T(8,128)S(1)} %add_add_fusion.1), channel_id=1, source_target_pairs={{0,24},{1,25},{2,26},{3,27},{4,28},{5,29},{6,30},{7,31},{8,16},{9,... | collective-permute-start | bytes 73736 | tf_op jit(solution)/shard_map/ppermute | solution.py:1101
  (4 other events, 8.8 us)
where the time goes:
time: 195 us; the launch traced here: 192 us
  Pallas kernels  93.6 us (48%)
  starting transfers between devices  47 us (24%)
  waiting for transfers between devices  36.4 us (19%)
  other arithmetic  12.6 us (6%)
    ppermute x42, starting transfers between devices, swap(): lax.ppermute(value, ('dp', 'fsdp'), [(place, place ^ mask) for place in r...  47 us
    ppermute x42, waiting for transfers between devices, swap(): lax.ppermute(value, ('dp', 'fsdp'), [(place, place ^ mask) for place in r...  36.4 us
    pallas_call x2, Pallas kernels, run_backward(): pl.pallas_call(functools.partial(backward_kernel, layer, widths, mesh_pla...  29.1 us
    pallas_call x1, Pallas kernels, run_middle(): pl.pallas_call(functools.partial(middle_kernel, widths, mesh_plan), in_sp...  28 us
    pallas_call x2, Pallas kernels, run_forward(): pl.pallas_call(functools.partial(forward_kernel, layer, widths, mesh_plan...  24.5 us
    add x5, other arithmetic, pick(): total = part if total is None else total + part  4.59 us
  transfers between devices with their start and end apart: 42, of which 21 were waited for; matrix products, arithmetic and copies ran while one was open for 4% of the time, Pallas kernels for 31%

commit v1 on v0

--- a/solution.py
+++ b/solution.py
@@ -721,10 +721,11 @@
 
 
 def run_backward(layer, widths, mesh_plan, blocks_like, saved, dmiddle, gains, core, before):
-    entry, _, qkv, mix, chance, weights = [in_hbm(item) for item in saved[:6]]
-    dmiddle = in_hbm(dmiddle)
+    entry, _, qkv, mix, chance = [in_hbm(item) for item in saved[:5]]
+    weights = saved[5]
     if layer > 0:
-        before = [in_hbm(item) for item in before]
+        dmiddle = in_hbm(dmiddle)
+        before = [in_hbm(before[0]), before[1]] + [in_hbm(item) for item in before[2:]]
     tokens = entry.shape[0]
     queries = chance.shape[3] // (HEADS // 2)
     short = tokens // CTX * queries
@@ -759,7 +760,7 @@
         in_specs = in_specs + [row_spec(D), whole_spec(before[1].shape), row_spec(FF)]
         in_specs.append(pl.BlockSpec(memory_space=pl.ANY))
         operands = operands + list(before)
-        outs.insert(0, (pltpu.HBM((tokens, D), f32), row_spec(D)))
+        outs.insert(0, (shape((tokens, D), f32), row_spec(D)))
         scratch = scratch + [
             pltpu.VMEM((tokens, D), b16),
             pltpu.VMEM((tokens, FF), b16),

time: 195 us -> 194 us (level)
    add x5, other arithmetic: 4.59 us -> 6.63 us  [pick(): total = part if total is None else total + part]
  transfers between devices with their start and end apart: 42 -> 42, of which waited for: 21 -> 20; matrix products, arithmetic and copies ran while one was open for 4% -> 4% of each run, Pallas kernels for 31% -> 30%
where the time goes in v1:
time: 194 us; the launch traced here: 191 us
  Pallas kernels  91.8 us (47%)
  starting transfers between devices  46.9 us (24%)
  waiting for transfers between devices  36.7 us (19%)
  other arithmetic  13.7 us (7%)
    ppermute x42, starting transfers between devices, swap(): lax.ppermute(value, ('dp', 'fsdp'), [(place, place ^ mask) for place in r...  46.9 us
    ppermute x42, waiting for transfers between devices, swap(): lax.ppermute(value, ('dp', 'fsdp'), [(place, place ^ mask) for place in r...  36.7 us
    pallas_call x1, Pallas kernels, run_middle(): pl.pallas_call(functools.partial(middle_kernel, widths, mesh_plan), in_sp...  28 us
    pallas_call x2, Pallas kernels, run_backward(): pl.pallas_call(functools.partial(backward_kernel, layer, widths, mesh_pla...  27.4 us
    pallas_call x2, Pallas kernels, run_forward(): pl.pallas_call(functools.partial(forward_kernel, layer, widths, mesh_plan...  24.4 us
    add x5, other arithmetic, pick(): total = part if total is None else total + part  6.63 us
  transfers between devices with their start and end apart: 42, of which 20 were waited for; matrix products, arithmetic and copies ran while one was open for 4% of the time, Pallas kernels for 30%

profile of v1, /device:TPU:0, one launch (start us, length us, event | category | flops | bytes accessed | tf_op | source)
XLA Modules:
  0.0 191.3 jit_solution(2572666085281022751)
XLA Ops:
  0.7 1.8 pack.1
  2.5 4.0 %collective-permute-start = (bf16[1,64,256]{2,1,0:T(8,128)(2,1)}, bf16[1,64,256]{2,1,0:T(8,128)(2,1)S(1)}, u32[]{:S(2)}, u32[]{:S(2)}) collective-permute-start(bf16[1,64,256]{2,1,0:T(8,128)(2,1)} %bitcast.127), channel_id=1, source_target_pairs={{0,16},{1,17},{2,18},{3,19},{4,20},{5,21},{6,22},{7,23},{8,24},{9,... | collective-permute-start | bytes 98312 | tf_op jit(solution)/shard_map/ppermute | solution.py:1102
  6.6 2.9 %collective-permute-start.2 = (bf16[1,64,768]{2,1,0:T(8,128)(2,1)}, bf16[1,64,768]{2,1,0:T(8,128)(2,1)S(1)}, u32[]{:S(2)}, u32[]{:S(2)}) collective-permute-start(bf16[1,64,768]{2,1,0:T(8,128)(2,1)} %bitcast.125), channel_id=1, source_target_pairs={{0,16},{1,17},{2,18},{3,19},{4,20},{5,21},{6,22},{7,23},{8,24},{9,... | collective-permute-start | bytes 294920 | tf_op jit(solution)/shard_map/ppermute | solution.py:1102
  9.5 1.8 first_statistics.1.refs_1_
  12.1 1.6 collective-permute-start.1
  13.7 1.6 collective-permute-done.7
  16.2 1.7 collective-permute-done.1
  18.0 2.5 %collective-permute-start.3 = (bf16[4,64,256]{2,1,0:T(8,128)(2,1)S(1)}, bf16[4,64,256]{2,1,0:T(8,128)(2,1)S(1)}, u32[]{:S(2)}, u32[]{:S(2)}) collective-permute-start(bf16[4,64,256]{2,1,0:T(8,128)(2,1)S(1)} %pad_maximum_fusion.7), channel_id=1, source_target_pairs={{0,6},{1,7},{2,4},{3,5},{4,2},{5,3},{6,0},{7,1},{8,14},{9,15},{10,... | collective-permute-start | bytes 393224 | tf_op jit(solution)/shard_map/ppermute | solution.py:1102
  21.6 1.6 collective-permute-start.10
  23.2 1.5 collective-permute-start.11
  25.4 2.4 %collective-permute-start.9 = (bf16[4,64,384]{2,1,0:T(8,128)(2,1)S(1)}, bf16[4,64,384]{2,1,0:T(8,128)(2,1)S(1)}, u32[]{:S(2)}, u32[]{:S(2)}) collective-permute-start(bf16[4,64,384]{2,1,0:T(8,128)(2,1)S(1)} %pad_maximum_fusion.5), channel_id=1, source_target_pairs={{0,6},{1,7},{2,4},{3,5},{4,2},{5,3},{6,0},{7,1},{8,14},{9,15},{10,... | collective-permute-start | bytes 589832 | tf_op jit(solution)/shard_map/ppermute | solution.py:1102
  29.1 3.4 %collective-permute-done.10 = bf16[4,64,384]{2,1,0:T(8,128)(2,1)S(1)} collective-permute-done((bf16[4,64,384]{2,1,0:T(8,128)(2,1)S(1)}, bf16[4,64,384]{2,1,0:T(8,128)(2,1)S(1)}, u32[]{:S(2)}, u32[]{:S(2)}) %collective-permute-start.10) | collective-permute-done | bytes 196640 | tf_op jit(solution)/shard_map/ppermute | solution.py:1102
  32.5 2.3 %collective-permute-done.11 = bf16[4,64,384]{2,1,0:T(8,128)(2,1)S(1)} collective-permute-done((bf16[4,64,384]{2,1,0:T(8,128)(2,1)S(1)}, bf16[4,64,384]{2,1,0:T(8,128)(2,1)S(1)}, u32[]{:S(2)}, u32[]{:S(2)}) %collective-permute-start.11) | collective-permute-done | bytes 196640 | tf_op jit(solution)/shard_map/ppermute | solution.py:1102
  36.7 1.5 collective-permute-start.15
  38.2 1.2 collective-permute-start.16
  39.5 10.2 %forward_part.2 = (f32[1536,256]{1,0:T(8,128)}, f32[1536,256]{1,0:T(8,128)}, bf16[1536,768]{1,0:T(8,128)(2,1)}, bf16[1536,256]{1,0:T(8,128)(2,1)}, bf16[16,2,96,...) custom-call(s32[16,32,96]{2,1,0:T(8,128)S(1)} %bitcast.104, bf16[16,64,256]{2,1,0:T(8,128)(2,1)S(1)} %pad_maximum_fusion.2.own_ref, ...), custom_call_target="tpu_custom_call" | custom-call | flops 2415919104 | bytes 9437184 | tf_op jit(solution)/shard_map/forward_part/pallas_call | solution.py:378
  49.6 14.3 %forward_part.3 = (f32[1536,256]{1,0:T(8,128)}, f32[1536,256]{1,0:T(8,128)}, bf16[1536,768]{1,0:T(8,128)(2,1)}, bf16[1536,256]{1,0:T(8,128)(2,1)}, bf16[16,2,96,...) custom-call(f32[1536,256]{1,0:T(8,128)} %get-tuple-element.137.sourc, ...), custom_call_target="tpu_custom_call" | custom-call | flops 2415919104 | bytes 9437184 | tf_op jit(solution)/shard_map/forward_part/pallas_call | solution.py:378
  64.4 3.4 %collective-permute-done.17.refs_2_ = bf16[16,64,768]{2,1,0:T(8,128)(2,1)S(1)} collective-permute-done((bf16[16,64,768]{2,1,0:T(8,128)(2,1)S(1)}, bf16[16,64,768]{2,1,0:T(8,128)(2,1)S(1)}, u32[]{:S(2)}, u32[]{:S(2)}) %collective-permute-start.17) | collective-permute-done | bytes 1572896 | tf_op jit(solution)/shard_map/ppermute | solution.py:1102
  67.8 28.0 %middle_part.1 = (f32[1536,256]{1,0:T(8,128)}, bf16[16,64,768]{2,1,0:T(8,128)(2,1)S(1)}, bf16[16,64,768]{2,1,0:T(8,128)(2,1)S(1)}, f32[4,256]{1,0:T(4,128)}, f32[1,1]{1,0:T(1,128)}, /*index=5*/f32[1,1]{1,0:T(1,128)}) custom-call(f32[1536,256]{1,0:T(8,128)S(1)} %copy-done.5, bf16[16,64,768]{2,1,0:T(8,128)(2,1)S(1)} %pad_maximum_fusion.refs_1_, ...), custom_call_target="tpu_custom_call" | custom-call | flops 19327352832 | bytes 18874368 | tf_op jit(solution)/shard_map/middle_part/pallas_call | solution.py:610
  96.0 3.4 %collective-permute-done.18 = bf16[16,64,768]{2,1,0:T(8,128)(2,1)} collective-permute-done((bf16[16,64,768]{2,1,0:T(8,128)(2,1)S(1)}, bf16[16,64,768]{2,1,0:T(8,128)(2,1)}, u32[]{:S(2)}, u32[]{:S(2)}) %collective-permute-start.18) | collective-permute-done | bytes 1572896 | tf_op jit(solution)/shard_map/ppermute | solution.py:1102
  99.4 2.8 %convert_add_fusion = (f32[1,4,64,768]{3,2,1,0:T(8,128)}, bf16[4,64,768]{2,1,0:T(8,128)(2,1)S(1)}, bf16[4,64,768]{2,1,0:T(8,128)(2,1)S(1)}, bf16[4,64,768]{2,1,0:T(8,128)(2,1)S(1)}) fusion(bf16[4,4,64,768]{3,2,1,0:T(8,128)(2,1)} %bitcast.12, s32[]{:T(128)S(6)} %select_n.355, bf16[4,4,64,768]{3,2,1,0:T(8,128)(2,1)S(1)} %bitcast.100, s32[]{:T(128)S(6)} %select_n.359, ...), kind=kLoop, calls=%fused_computation.5 | loop fusion | flops 2949120 | bytes 5111824 | tf_op jit(solution)/shard_map/add | solution.py:1167
  102.9 1.5 collective-permute-start.20
  104.4 1.2 collective-permute-start.21
  105.7 15.4 %backward_part.2 = (f32[1536,256]{1,0:T(8,128)S(1)}, bf16[16,64,384]{2,1,0:T(8,128)(2,1)S(1)}, bf16[16,64,384]{2,1,0:T(8,128)(2,1)S(1)}, f32[2,256]{1,0:T(2,128)}) custom-call(f32[1536,256]{1,0:T(8,128)} %get-tuple-element.147.refs_0_, bf16[1536,768]{1,0:T(8,128)(2,1)} %get-tuple-element.148.refs_1_, bf16[1536,256]{1,0:T(8,128)(2,1)} %get-tuple-element.149.refs_2_, ...), custom_call_target="tpu_custom_call" | custom-call | flops 7247757312 | bytes 14155776 | tf_op jit(solution)/shard_map/backward_part/pallas_call | solution.py:773
  121.1 1.9 %collective-permute-done.21 = bf16[4,64,768]{2,1,0:T(8,128)(2,1)} collective-permute-done((bf16[4,64,768]{2,1,0:T(8,128)(2,1)S(1)}, bf16[4,64,768]{2,1,0:T(8,128)(2,1)}, u32[]{:S(2)}, u32[]{:S(2)}) %collective-permute-start.21) | collective-permute-done | bytes 393248 | tf_op jit(solution)/shard_map/ppermute | solution.py:1102
  123.0 2.4 %convert_add_fusion.2 = (f32[1,2,64,768]{3,2,1,0:T(8,128)}, bf16[2,64,768]{2,1,0:T(8,128)(2,1)S(1)}) fusion(f32[2,2,64,768]{3,2,1,0:T(8,128)} %bitcast.106, s32[]{:T(128)S(6)} %select_n.356, bf16[2,2,64,768]{3,2,1,0:T(8,128)(2,1)} %bitcast.19, bf16[2,2,64,768]{3,2,1,0:T(8,128)(2,1)} %bitcast.18, bf16[2,2,64,768]{3,2,1,0:T(8,128)(2,1)} %bitcast.17, ...), kind=kLoop, calls=%fused_computation.16 | loop fusion | flops 1277952 | bytes 2555912 | tf_op jit(solution)/shard_map/add | solution.py:1167
  125.5 1.5 fusion.7
  127.5 1.2 collective-permute-start.24
  128.7 1.6 collective-permute-start.25
  131.0 12.0 %backward_part.3 = (bf16[16,64,256]{2,1,0:T(8,128)(2,1)S(1)}, bf16[16,64,256]{2,1,0:T(8,128)(2,1)S(1)}, f32[2,256]{1,0:T(2,128)}) custom-call(f32[1536,256]{1,0:T(8,128)} %get-tuple-element.166.refs_0_, bf16[1536,768]{1,0:T(8,128)(2,1)} %get-tuple-element.167.refs_1_, bf16[1536,256]{1,0:T(8,128)(2,1)} %get-tuple-element.168.refs_2_, ...), custom_call_target="tpu_custom_call" | custom-call | flops 4831838208 | bytes 12582912 | tf_op jit(solution)/shard_map/backward_part/pallas_call | solution.py:773
  143.8 1.2 fusion.12
  145.1 1.6 collective-permute-start.27
  147.7 1.5 collective-permute-start.30
  149.2 1.2 collective-permute-start.31
  150.5 2.4 %collective-permute-start.33 = (bf16[1,64,1152]{2,1,0:T(8,128)(2,1)S(1)}, bf16[1,64,1152]{2,1,0:T(8,128)(2,1)S(1)}, u32[]{:S(2)}, u32[]{:S(2)}) collective-permute-start(bf16[1,64,1152]{2,1,0:T(8,128)(2,1)S(1)} %pad_maximum_fusion.6), channel_id=1, source_target_pairs={{0,16},{1,17},{2,18},{3,19},{4,20},{5,21},{6,22},{7,23},{8,24},{9,... | collective-permute-start | bytes 442376 | tf_op jit(solution)/shard_map/ppermute | solution.py:1102
  153.9 2.6 %collective-permute-done.31 = bf16[4,64,256]{2,1,0:T(8,128)(2,1)S(1)} collective-permute-done((bf16[4,64,256]{2,1,0:T(8,128)(2,1)S(1)}, bf16[4,64,256]{2,1,0:T(8,128)(2,1)S(1)}, u32[]{:S(2)}, u32[]{:S(2)}) %collective-permute-start.31) | collective-permute-done | bytes 131104 | tf_op jit(solution)/shard_map/ppermute | solution.py:1102
  157.2 2.9 %collective-permute-done.33 = bf16[1,64,1152]{2,1,0:T(8,128)(2,1)S(1)} collective-permute-done((bf16[1,64,1152]{2,1,0:T(8,128)(2,1)S(1)}, bf16[1,64,1152]{2,1,0:T(8,128)(2,1)S(1)}, u32[]{:S(2)}, u32[]{:S(2)}) %collective-permute-start.33) | collective-permute-done | bytes 147488 | tf_op jit(solution)/shard_map/ppermute | solution.py:1102
  160.1 1.3 collective-permute-done.32
  163.2 3.2 %early_statistics.1.early_ref = f32[48,128]{1,0:T(8,128)} custom-call(f32[64,1152]{1,0:T(8,128)} %fusion.3.refs_0_.refs_1_, f32[1,128]{1,0:T(1,128)} %first_statistics.1.refs_1_, f32[4,256]{1,0:T(4,128)} %get-tuple-element.190.refs_2_, f32[2,256]{1,0:T(2,128)} %get-tuple-element.191.refs_3_, f32[1,1]{1,0:T(1,128)} %get-tuple-element.192.refs_4_, ...), custom_call_target="tpu_custom_call" | custom-call | tf_op jit(solution)/shard_map/early_statistics/pallas_call | solution.py:972
  167.0 1.7 late_statistics.1
  168.7 1.4 collective-permute-done.35
  172.1 1.5 collective-permute-start.37
  175.9 2.4 %collective-permute-done.38 = f32[48,128]{1,0:T(8,128)S(1)} collective-permute-done((f32[48,128]{1,0:T(8,128)S(1)}, f32[48,128]{1,0:T(8,128)S(1)}, u32[]{:S(2)}, u32[]{:S(2)}) %collective-permute-start.38) | collective-permute-done | bytes 24608 | tf_op jit(solution)/shard_map/ppermute | solution.py:1102
  178.4 1.9 %collective-permute-start.39 = (f32[48,128]{1,0:T(8,128)S(1)}, f32[48,128]{1,0:T(8,128)S(1)}, u32[]{:S(2)}, u32[]{:S(2)}) collective-permute-start(f32[48,128]{1,0:T(8,128)S(1)} %add_add_fusion.1), channel_id=1, source_target_pairs={{0,8},{1,9},{2,10},{3,11},{4,12},{5,13},{6,14},{7,15},{8,0},{9,1},... | collective-permute-start | bytes 73736 | tf_op jit(solution)/shard_map/ppermute | solution.py:1102
  181.2 1.6 collective-permute-start.41
  182.9 2.2 %collective-permute-done.40 = f32[48,128]{1,0:T(8,128)S(1)} collective-permute-done((f32[48,128]{1,0:T(8,128)S(1)}, f32[48,128]{1,0:T(8,128)S(1)}, u32[]{:S(2)}, u32[]{:S(2)}) %collective-permute-start.40) | collective-permute-done | bytes 24608 | tf_op jit(solution)/shard_map/ppermute | solution.py:1102
  185.1 1.8 collective-permute-done.41
  187.5 3.5 %update.1 = (f32[1,1]{1,0:T(1,128)}, f32[1,1]{1,0:T(1,128)}, f32[1,1]{1,0:T(1,128)}, f32[64,128]{1,0:T(8,128)}, f32[64,128]{1,0:T(8,128)}, /*index=5*/f32[1,128]...) custom-call(f32[48,128]{1,0:T(8,128)} %add_add_fusion.refs_0_, ...), custom_call_target="tpu_custom_call" | custom-call | tf_op jit(solution)/shard_map/update/pallas_call | solution.py:1091
  (109 shorter events, 21.2 us)
Async XLA Ops:
  2.5 15.4 %copy-start.13 = (bf16[64,768]{1,0:T(8,128)(2,1)S(1)}, bf16[64,768]{1,0:T(8,128)(2,1)}, u32[]{:S(2)}) copy-start(bf16[64,768]{1,0:T(8,128)(2,1)} %get-tuple-element.130) | copy-start | bytes 294916
  2.5 8.8 %collective-permute-start = (bf16[1,64,256]{2,1,0:T(8,128)(2,1)}, bf16[1,64,256]{2,1,0:T(8,128)(2,1)S(1)}, u32[]{:S(2)}, u32[]{:S(2)}) collective-permute-start(bf16[1,64,256]{2,1,0:T(8,128)(2,1)} %bitcast.127), channel_id=1, source_target_pairs={{0,16},{1,17},{2,18},{3,19},{4,20},{5,21},{6,22},{7,23},{8,24},{9,... | collective-permute-start | bytes 98312 | tf_op jit(solution)/shard_map/ppermute | solution.py:1102
  6.6 8.7 %collective-permute-start.7 = (bf16[1,64,384]{2,1,0:T(8,128)(2,1)}, bf16[1,64,384]{2,1,0:T(8,128)(2,1)S(1)}, u32[]{:S(2)}, u32[]{:S(2)}) collective-permute-start(bf16[1,64,384]{2,1,0:T(8,128)(2,1)} %bitcast.126), channel_id=1, source_target_pairs={{0,16},{1,17},{2,18},{3,19},{4,20},{5,21},{6,22},{7,23},{8,24},{9,... | collective-permute-start | bytes 147464 | tf_op jit(solution)/shard_map/ppermute | solution.py:1102
  6.6 11.3 %collective-permute-start.2 = (bf16[1,64,768]{2,1,0:T(8,128)(2,1)}, bf16[1,64,768]{2,1,0:T(8,128)(2,1)S(1)}, u32[]{:S(2)}, u32[]{:S(2)}) collective-permute-start(bf16[1,64,768]{2,1,0:T(8,128)(2,1)} %bitcast.125), channel_id=1, source_target_pairs={{0,16},{1,17},{2,18},{3,19},{4,20},{5,21},{6,22},{7,23},{8,24},{9,... | collective-permute-start | bytes 294920 | tf_op jit(solution)/shard_map/ppermute | solution.py:1102
  12.1 5.8 %collective-permute-start.1 = (bf16[2,64,256]{2,1,0:T(8,128)(2,1)S(1)}, bf16[2,64,256]{2,1,0:T(8,128)(2,1)S(1)}, u32[]{:S(2)}, u32[]{:S(2)}) collective-permute-start(bf16[2,64,256]{2,1,0:T(8,128)(2,1)S(1)} %pad_maximum_fusion.9), channel_id=1, source_target_pairs={{0,8},{1,9},{2,10},{3,11},{4,12},{5,13},{6,14},{7,15},{8,0},{9,1},... | collective-permute-start | bytes 196616 | tf_op jit(solution)/shard_map/ppermute | solution.py:1102
  16.1 5.4 %collective-permute-start.8 = (bf16[2,64,384]{2,1,0:T(8,128)(2,1)S(1)}, bf16[2,64,384]{2,1,0:T(8,128)(2,1)S(1)}, u32[]{:S(2)}, u32[]{:S(2)}) collective-permute-start(bf16[2,64,384]{2,1,0:T(8,128)(2,1)S(1)} %pad_maximum_fusion.8), channel_id=1, source_target_pairs={{0,8},{1,9},{2,10},{3,11},{4,12},{5,13},{6,14},{7,15},{8,0},{9,1},... | collective-permute-start | bytes 294920 | tf_op jit(solution)/shard_map/ppermute | solution.py:1102
  18.0 7.4 %collective-permute-start.3 = (bf16[4,64,256]{2,1,0:T(8,128)(2,1)S(1)}, bf16[4,64,256]{2,1,0:T(8,128)(2,1)S(1)}, u32[]{:S(2)}, u32[]{:S(2)}) collective-permute-start(bf16[4,64,256]{2,1,0:T(8,128)(2,1)S(1)} %pad_maximum_fusion.7), channel_id=1, source_target_pairs={{0,6},{1,7},{2,4},{3,5},{4,2},{5,3},{6,0},{7,1},{8,14},{9,15},{10,... | collective-permute-start | bytes 393224 | tf_op jit(solution)/shard_map/ppermute | solution.py:1102
  20.5 7.8 %collective-permute-start.4 = (bf16[4,64,256]{2,1,0:T(8,128)(2,1)S(1)}, bf16[4,64,256]{2,1,0:T(8,128)(2,1)S(1)}, u32[]{:S(2)}, u32[]{:S(2)}) collective-permute-start(bf16[4,64,256]{2,1,0:T(8,128)(2,1)S(1)} %pad_maximum_fusion.7), channel_id=1, source_target_pairs={{0,4},{1,5},{2,6},{3,7},{4,0},{5,1},{6,2},{7,3},{8,12},{9,13},{10,... | collective-permute-start | bytes 393224 | tf_op jit(solution)/shard_map/ppermute | solution.py:1102
  21.1 7.2 %collective-permute-start.5 = (bf16[4,64,256]{2,1,0:T(8,128)(2,1)S(1)}, bf16[4,64,256]{2,1,0:T(8,128)(2,1)S(1)}, u32[]{:S(2)}, u32[]{:S(2)}) collective-permute-start(bf16[4,64,256]{2,1,0:T(8,128)(2,1)S(1)} %pad_maximum_fusion.7), channel_id=1, source_target_pairs={{0,2},{1,3},{2,0},{3,1},{4,6},{5,7},{6,4},{7,5},{8,10},{9,11},{10,... | collective-permute-start | bytes 393224 | tf_op jit(solution)/shard_map/ppermute | solution.py:1102
  21.6 10.9 %collective-permute-start.10 = (bf16[4,64,384]{2,1,0:T(8,128)(2,1)S(1)}, bf16[4,64,384]{2,1,0:T(8,128)(2,1)S(1)}, u32[]{:S(2)}, u32[]{:S(2)}) collective-permute-start(bf16[4,64,384]{2,1,0:T(8,128)(2,1)S(1)} %pad_maximum_fusion.5), channel_id=1, source_target_pairs={{0,4},{1,5},{2,6},{3,7},{4,0},{5,1},{6,2},{7,3},{8,12},{9,13},{10,... | collective-permute-start | bytes 589832 | tf_op jit(solution)/shard_map/ppermute | solution.py:1102
  23.2 11.5 %collective-permute-start.11 = (bf16[4,64,384]{2,1,0:T(8,128)(2,1)S(1)}, bf16[4,64,384]{2,1,0:T(8,128)(2,1)S(1)}, u32[]{:S(2)}, u32[]{:S(2)}) collective-permute-start(bf16[4,64,384]{2,1,0:T(8,128)(2,1)S(1)} %pad_maximum_fusion.5), channel_id=1, source_target_pairs={{0,2},{1,3},{2,0},{3,1},{4,6},{5,7},{6,4},{7,5},{8,10},{9,11},{10,... | collective-permute-start | bytes 589832 | tf_op jit(solution)/shard_map/ppermute | solution.py:1102
  25.4 9.3 %collective-permute-start.9 = (bf16[4,64,384]{2,1,0:T(8,128)(2,1)S(1)}, bf16[4,64,384]{2,1,0:T(8,128)(2,1)S(1)}, u32[]{:S(2)}, u32[]{:S(2)}) collective-permute-start(bf16[4,64,384]{2,1,0:T(8,128)(2,1)S(1)} %pad_maximum_fusion.5), channel_id=1, source_target_pairs={{0,6},{1,7},{2,4},{3,5},{4,2},{5,3},{6,0},{7,1},{8,14},{9,15},{10,... | collective-permute-start | bytes 589832 | tf_op jit(solution)/shard_map/ppermute | solution.py:1102
  28.4 6.6 %collective-permute-start.6 = (bf16[16,64,256]{2,1,0:T(8,128)(2,1)S(1)}, bf16[16,64,256]{2,1,0:T(8,128)(2,1)S(1)}, u32[]{:S(2)}, u32[]{:S(2)}) collective-permute-start(bf16[16,64,256]{2,1,0:T(8,128)(2,1)S(1)} %pad_maximum_fusion.2.own_ref), channel_id=1, source_target_pairs={{0,1},{1,0},{2,3},{3,2},{4,5},{5,4},{6,7},{7,6},{8,9},{9,8},{10,11... | collective-permute-start | bytes 1572872 | tf_op jit(solution)/shard_map/ppermute | solution.py:1102
  28.5 7.3 %collective-permute-start.13 = (bf16[2,64,768]{2,1,0:T(8,128)(2,1)S(1)}, bf16[2,64,768]{2,1,0:T(8,128)(2,1)S(1)}, u32[]{:S(2)}, u32[]{:S(2)}) collective-permute-start(bf16[2,64,768]{2,1,0:T(8,128)(2,1)S(1)} %pad_maximum_fusion.4), channel_id=1, source_target_pairs={{0,8},{1,9},{2,10},{3,11},{4,12},{5,13},{6,14},{7,15},{8,0},{9,1},... | collective-permute-start | bytes 589832 | tf_op jit(solution)/shard_map/ppermute | solution.py:1102
  34.9 4.6 %copy-start = (f32[7,256]{1,0:T(8,128)S(1)}, f32[7,256]{1,0:T(8,128)}, u32[]{:S(2)}) copy-start(f32[7,256]{1,0:T(8,128)} %refs_21_.1) | copy-start | bytes 21508
  34.9 4.6 %copy-start.2 = (s32[16,96,32]{1,2,0:T(8,128)S(1)}, s32[16,96,32]{1,2,0:T(8,128)}, u32[]{:S(2)}) copy-start(s32[16,96,32]{1,2,0:T(8,128)} %param.24) | copy-start | bytes 589828
  35.1 14.6 %collective-permute-start.12 = (bf16[16,64,384]{2,1,0:T(8,128)(2,1)S(1)}, bf16[16,64,384]{2,1,0:T(8,128)(2,1)S(1)}, u32[]{:S(2)}, u32[]{:S(2)}) collective-permute-start(bf16[16,64,384]{2,1,0:T(8,128)(2,1)S(1)} %pad_maximum_fusion.1.own_ref), channel_id=1, source_target_pairs={{0,1},{1,0},{2,3},{3,2},{4,5},{5,4},{6,7},{7,6},{8,9},{9,8},{10,11... | collective-permute-start | bytes 2359304 | tf_op jit(solution)/shard_map/ppermute | solution.py:1102
  35.9 28.0 %collective-permute-start.14 = (bf16[4,64,768]{2,1,0:T(8,128)(2,1)S(1)}, bf16[4,64,768]{2,1,0:T(8,128)(2,1)S(1)}, u32[]{:S(2)}, u32[]{:S(2)}) collective-permute-start(bf16[4,64,768]{2,1,0:T(8,128)(2,1)S(1)} %pad_maximum_fusion.3), channel_id=1, source_target_pairs={{0,2},{1,3},{2,0},{3,1},{4,6},{5,7},{6,4},{7,5},{8,10},{9,11},{10,... | collective-permute-start | bytes 1179656 | tf_op jit(solution)/shard_map/ppermute | solution.py:1102
  36.7 27.2 %collective-permute-start.15 = (bf16[4,64,768]{2,1,0:T(8,128)(2,1)S(1)}, bf16[4,64,768]{2,1,0:T(8,128)(2,1)S(1)}, u32[]{:S(2)}, u32[]{:S(2)}) collective-permute-start(bf16[4,64,768]{2,1,0:T(8,128)(2,1)S(1)} %pad_maximum_fusion.3), channel_id=1, source_target_pairs={{0,4},{1,5},{2,6},{3,7},{4,0},{5,1},{6,2},{7,3},{8,12},{9,13},{10,... | collective-permute-start | bytes 1179656 | tf_op jit(solution)/shard_map/ppermute | solution.py:1102
  38.2 25.7 %collective-permute-start.16 = (bf16[4,64,768]{2,1,0:T(8,128)(2,1)S(1)}, bf16[4,64,768]{2,1,0:T(8,128)(2,1)S(1)}, u32[]{:S(2)}, u32[]{:S(2)}) collective-permute-start(bf16[4,64,768]{2,1,0:T(8,128)(2,1)S(1)} %pad_maximum_fusion.3), channel_id=1, source_target_pairs={{0,6},{1,7},{2,4},{3,5},{4,2},{5,3},{6,0},{7,1},{8,14},{9,15},{10,... | collective-permute-start | bytes 1179656 | tf_op jit(solution)/shard_map/ppermute | solution.py:1102
  64.3 3.5 %collective-permute-start.17 = (bf16[16,64,768]{2,1,0:T(8,128)(2,1)S(1)}, bf16[16,64,768]{2,1,0:T(8,128)(2,1)S(1)}, u32[]{:S(2)}, u32[]{:S(2)}) collective-permute-start(bf16[16,64,768]{2,1,0:T(8,128)(2,1)S(1)} %pad_maximum_fusion.refs_1_), channel_id=1, source_target_pairs={{0,1},{1,0},{2,3},{3,2},{4,5},{5,4},{6,7},{7,6},{8,9},{9,8},{10,11... | collective-permute-start | bytes 4718600 | tf_op jit(solution)/shard_map/ppermute | solution.py:1102
  95.8 3.5 %collective-permute-start.18 = (bf16[16,64,768]{2,1,0:T(8,128)(2,1)S(1)}, bf16[16,64,768]{2,1,0:T(8,128)(2,1)}, u32[]{:S(2)}, u32[]{:S(2)}) collective-permute-start(bf16[16,64,768]{2,1,0:T(8,128)(2,1)S(1)} %get-tuple-element.146), channel_id=1, source_target_pairs={{0,1},{1,0},{2,3},{3,2},{4,5},{5,4},{6,7},{7,6},{8,9},{9,8},{10,11... | collective-permute-start | bytes 4718600 | tf_op jit(solution)/shard_map/ppermute | solution.py:1102
  99.4 6.3 %copy-start.6 = (bf16[256,2048]{1,0:T(8,128)(2,1)S(1)}, bf16[256,2048]{1,0:T(8,128)(2,1)}, u32[]{:S(2)}) copy-start(bf16[256,2048]{1,0:T(8,128)(2,1)} %get-tuple-element.154.refs_9_) | copy-start | bytes 3145732
  99.4 6.3 %copy-start.7 = (bf16[256,1024]{1,0:T(8,128)(2,1)S(1)}, bf16[256,1024]{1,0:T(8,128)(2,1)}, u32[]{:S(2)}) copy-start(bf16[256,1024]{1,0:T(8,128)(2,1)} %get-tuple-element.153.refs_5_) | copy-start | bytes 1572868
  102.2 18.9 %collective-permute-start.19 = (bf16[4,64,768]{2,1,0:T(8,128)(2,1)S(1)}, bf16[4,64,768]{2,1,0:T(8,128)(2,1)}, u32[]{:S(2)}, u32[]{:S(2)}) collective-permute-start(bf16[4,64,768]{2,1,0:T(8,128)(2,1)S(1)} %get-tuple-element.160), channel_id=1, source_target_pairs={{0,2},{1,3},{2,0},{3,1},{4,6},{5,7},{6,4},{7,5},{8,10},{9,11},{10,... | collective-permute-start | bytes 1179656 | tf_op jit(solution)/shard_map/ppermute | solution.py:1102
  102.9 18.2 %collective-permute-start.20 = (bf16[4,64,768]{2,1,0:T(8,128)(2,1)S(1)}, bf16[4,64,768]{2,1,0:T(8,128)(2,1)}, u32[]{:S(2)}, u32[]{:S(2)}) collective-permute-start(bf16[4,64,768]{2,1,0:T(8,128)(2,1)S(1)} %get-tuple-element.161), channel_id=1, source_target_pairs={{0,4},{1,5},{2,6},{3,7},{4,0},{5,1},{6,2},{7,3},{8,12},{9,13},{10,... | collective-permute-start | bytes 1179656 | tf_op jit(solution)/shard_map/ppermute | solution.py:1102
  104.4 18.6 %collective-permute-start.21 = (bf16[4,64,768]{2,1,0:T(8,128)(2,1)S(1)}, bf16[4,64,768]{2,1,0:T(8,128)(2,1)}, u32[]{:S(2)}, u32[]{:S(2)}) collective-permute-start(bf16[4,64,768]{2,1,0:T(8,128)(2,1)S(1)} %get-tuple-element.162), channel_id=1, source_target_pairs={{0,6},{1,7},{2,4},{3,5},{4,2},{5,3},{6,0},{7,1},{8,14},{9,15},{10,... | collective-permute-start | bytes 1179656 | tf_op jit(solution)/shard_map/ppermute | solution.py:1102
  123.0 2.4 %collective-permute-start.22 = (bf16[16,64,384]{2,1,0:T(8,128)(2,1)S(1)}, bf16[16,64,384]{2,1,0:T(8,128)(2,1)}, u32[]{:S(2)}, u32[]{:S(2)}) collective-permute-start(bf16[16,64,384]{2,1,0:T(8,128)(2,1)S(1)} %get-tuple-element.172), channel_id=1, source_target_pairs={{0,1},{1,0},{2,3},{3,2},{4,5},{5,4},{6,7},{7,6},{8,9},{9,8},{10,11... | collective-permute-start | bytes 2359304 | tf_op jit(solution)/shard_map/ppermute | solution.py:1102
  125.4 5.6 %copy-start.8 = (bf16[256,1024]{1,0:T(8,128)(2,1)S(1)}, bf16[256,1024]{1,0:T(8,128)(2,1)}, u32[]{:S(2)}) copy-start(bf16[256,1024]{1,0:T(8,128)(2,1)} %get-tuple-element.174.refs_5_) | copy-start | bytes 1572868
  126.9 16.1 %collective-permute-start.23 = (bf16[2,64,768]{2,1,0:T(8,128)(2,1)S(1)}, bf16[2,64,768]{2,1,0:T(8,128)(2,1)S(1)}, u32[]{:S(2)}, u32[]{:S(2)}) collective-permute-start(bf16[2,64,768]{2,1,0:T(8,128)(2,1)S(1)} %get-tuple-element.177), channel_id=1, source_target_pairs={{0,8},{1,9},{2,10},{3,11},{4,12},{5,13},{6,14},{7,15},{8,0},{9,1},... | collective-permute-start | bytes 589832 | tf_op jit(solution)/shard_map/ppermute | solution.py:1102
  127.5 15.5 %collective-permute-start.24 = (bf16[4,64,384]{2,1,0:T(8,128)(2,1)S(1)}, bf16[4,64,384]{2,1,0:T(8,128)(2,1)S(1)}, u32[]{:S(2)}, u32[]{:S(2)}) collective-permute-start(bf16[4,64,384]{2,1,0:T(8,128)(2,1)S(1)} %get-tuple-element.178), channel_id=1, source_target_pairs={{0,2},{1,3},{2,0},{3,1},{4,6},{5,7},{6,4},{7,5},{8,10},{9,11},{10,... | collective-permute-start | bytes 589832 | tf_op jit(solution)/shard_map/ppermute | solution.py:1102
  128.7 14.3 %collective-permute-start.25 = (bf16[4,64,384]{2,1,0:T(8,128)(2,1)S(1)}, bf16[4,64,384]{2,1,0:T(8,128)(2,1)S(1)}, u32[]{:S(2)}, u32[]{:S(2)}) collective-permute-start(bf16[4,64,384]{2,1,0:T(8,128)(2,1)S(1)} %get-tuple-element.179), channel_id=1, source_target_pairs={{0,4},{1,5},{2,6},{3,7},{4,0},{5,1},{6,2},{7,3},{8,12},{9,13},{10,... | collective-permute-start | bytes 589832 | tf_op jit(solution)/shard_map/ppermute | solution.py:1102
  130.3 12.7 %collective-permute-start.26 = (bf16[4,64,384]{2,1,0:T(8,128)(2,1)S(1)}, bf16[4,64,384]{2,1,0:T(8,128)(2,1)S(1)}, u32[]{:S(2)}, u32[]{:S(2)}) collective-permute-start(bf16[4,64,384]{2,1,0:T(8,128)(2,1)S(1)} %get-tuple-element.180), channel_id=1, source_target_pairs={{0,6},{1,7},{2,4},{3,5},{4,2},{5,3},{6,0},{7,1},{8,14},{9,15},{10,... | collective-permute-start | bytes 589832 | tf_op jit(solution)/shard_map/ppermute | solution.py:1102
  143.8 2.9 %collective-permute-start.28 = (bf16[16,64,256]{2,1,0:T(8,128)(2,1)S(1)}, bf16[16,64,256]{2,1,0:T(8,128)(2,1)S(1)}, u32[]{:S(2)}, u32[]{:S(2)}) collective-permute-start(bf16[16,64,256]{2,1,0:T(8,128)(2,1)S(1)} %get-tuple-element.186), channel_id=1, source_target_pairs={{0,1},{1,0},{2,3},{3,2},{4,5},{5,4},{6,7},{7,6},{8,9},{9,8},{10,11... | collective-permute-start | bytes 1572872 | tf_op jit(solution)/shard_map/ppermute | solution.py:1102
  145.1 5.4 %collective-permute-start.27 = (bf16[2,64,384]{2,1,0:T(8,128)(2,1)S(1)}, bf16[2,64,384]{2,1,0:T(8,128)(2,1)S(1)}, u32[]{:S(2)}, u32[]{:S(2)}) collective-permute-start(bf16[2,64,384]{2,1,0:T(8,128)(2,1)S(1)} %get-tuple-element.244), channel_id=1, source_target_pairs={{0,8},{1,9},{2,10},{3,11},{4,12},{5,13},{6,14},{7,15},{8,0},{9,1},... | collective-permute-start | bytes 294920 | tf_op jit(solution)/shard_map/ppermute | solution.py:1102
  146.9 6.0 %collective-permute-start.29 = (bf16[4,64,256]{2,1,0:T(8,128)(2,1)S(1)}, bf16[4,64,256]{2,1,0:T(8,128)(2,1)S(1)}, u32[]{:S(2)}, u32[]{:S(2)}) collective-permute-start(bf16[4,64,256]{2,1,0:T(8,128)(2,1)S(1)} %get-tuple-element.243), channel_id=1, source_target_pairs={{0,2},{1,3},{2,0},{3,1},{4,6},{5,7},{6,4},{7,5},{8,10},{9,11},{10,... | collective-permute-start | bytes 393224 | tf_op jit(solution)/shard_map/ppermute | solution.py:1102
  147.7 6.3 %collective-permute-start.30 = (bf16[4,64,256]{2,1,0:T(8,128)(2,1)S(1)}, bf16[4,64,256]{2,1,0:T(8,128)(2,1)S(1)}, u32[]{:S(2)}, u32[]{:S(2)}) collective-permute-start(bf16[4,64,256]{2,1,0:T(8,128)(2,1)S(1)} %get-tuple-element.242), channel_id=1, source_target_pairs={{0,4},{1,5},{2,6},{3,7},{4,0},{5,1},{6,2},{7,3},{8,12},{9,13},{10,... | collective-permute-start | bytes 393224 | tf_op jit(solution)/shard_map/ppermute | solution.py:1102
  149.2 7.4 %collective-permute-start.31 = (bf16[4,64,256]{2,1,0:T(8,128)(2,1)S(1)}, bf16[4,64,256]{2,1,0:T(8,128)(2,1)S(1)}, u32[]{:S(2)}, u32[]{:S(2)}) collective-permute-start(bf16[4,64,256]{2,1,0:T(8,128)(2,1)S(1)} %get-tuple-element.241), channel_id=1, source_target_pairs={{0,6},{1,7},{2,4},{3,5},{4,2},{5,3},{6,0},{7,1},{8,14},{9,15},{10,... | collective-permute-start | bytes 393224 | tf_op jit(solution)/shard_map/ppermute | solution.py:1102
  150.5 9.6 %collective-permute-start.33 = (bf16[1,64,1152]{2,1,0:T(8,128)(2,1)S(1)}, bf16[1,64,1152]{2,1,0:T(8,128)(2,1)S(1)}, u32[]{:S(2)}, u32[]{:S(2)}) collective-permute-start(bf16[1,64,1152]{2,1,0:T(8,128)(2,1)S(1)} %pad_maximum_fusion.6), channel_id=1, source_target_pairs={{0,16},{1,17},{2,18},{3,19},{4,20},{5,21},{6,22},{7,23},{8,24},{9,... | collective-permute-start | bytes 442376 | tf_op jit(solution)/shard_map/ppermute | solution.py:1102
  156.6 4.8 %collective-permute-start.32 = (bf16[2,64,256]{2,1,0:T(8,128)(2,1)S(1)}, bf16[2,64,256]{2,1,0:T(8,128)(2,1)S(1)}, u32[]{:S(2)}, u32[]{:S(2)}) collective-permute-start(bf16[2,64,256]{2,1,0:T(8,128)(2,1)S(1)} %get-tuple-element.251), channel_id=1, source_target_pairs={{0,8},{1,9},{2,10},{3,11},{4,12},{5,13},{6,14},{7,15},{8,0},{9,1},... | collective-permute-start | bytes 196616 | tf_op jit(solution)/shard_map/ppermute | solution.py:1102
  161.4 5.0 %collective-permute-start.34 = (bf16[1,64,256]{2,1,0:T(8,128)(2,1)S(1)}, bf16[1,64,256]{2,1,0:T(8,128)(2,1)S(1)}, u32[]{:S(2)}, u32[]{:S(2)}) collective-permute-start(bf16[1,64,256]{2,1,0:T(8,128)(2,1)S(1)} %fusion.15), channel_id=1, source_target_pairs={{0,16},{1,17},{2,18},{3,19},{4,20},{5,21},{6,22},{7,23},{8,24},{9,... | collective-permute-start | bytes 98312 | tf_op jit(solution)/shard_map/ppermute | solution.py:1102
  168.7 1.4 collective-permute-start.35
  170.9 3.8 %collective-permute-start.36 = (f32[48,128]{1,0:T(8,128)S(1)}, f32[48,128]{1,0:T(8,128)S(1)}, u32[]{:S(2)}, u32[]{:S(2)}) collective-permute-start(f32[48,128]{1,0:T(8,128)S(1)} %select_add_fusion), channel_id=1, source_target_pairs={{0,2},{1,3},{2,0},{3,1},{4,6},{5,7},{6,4},{7,5},{8,10},{9,11},{10,... | collective-permute-start | bytes 73736 | tf_op jit(solution)/shard_map/ppermute | solution.py:1102
  172.1 3.8 %collective-permute-start.37 = (f32[48,128]{1,0:T(8,128)S(1)}, f32[48,128]{1,0:T(8,128)S(1)}, u32[]{:S(2)}, u32[]{:S(2)}) collective-permute-start(f32[48,128]{1,0:T(8,128)S(1)} %select_add_fusion), channel_id=1, source_target_pairs={{0,4},{1,5},{2,6},{3,7},{4,0},{5,1},{6,2},{7,3},{8,12},{9,13},{10,... | collective-permute-start | bytes 73736 | tf_op jit(solution)/shard_map/ppermute | solution.py:1102
  173.6 4.7 %collective-permute-start.38 = (f32[48,128]{1,0:T(8,128)S(1)}, f32[48,128]{1,0:T(8,128)S(1)}, u32[]{:S(2)}, u32[]{:S(2)}) collective-permute-start(f32[48,128]{1,0:T(8,128)S(1)} %select_add_fusion), channel_id=1, source_target_pairs={{0,6},{1,7},{2,4},{3,5},{4,2},{5,3},{6,0},{7,1},{8,14},{9,15},{10,... | collective-permute-start | bytes 73736 | tf_op jit(solution)/shard_map/ppermute | solution.py:1102
  178.4 4.5 %collective-permute-start.39 = (f32[48,128]{1,0:T(8,128)S(1)}, f32[48,128]{1,0:T(8,128)S(1)}, u32[]{:S(2)}, u32[]{:S(2)}) collective-permute-start(f32[48,128]{1,0:T(8,128)S(1)} %add_add_fusion.1), channel_id=1, source_target_pairs={{0,8},{1,9},{2,10},{3,11},{4,12},{5,13},{6,14},{7,15},{8,0},{9,1},... | collective-permute-start | bytes 73736 | tf_op jit(solution)/shard_map/ppermute | solution.py:1102
  180.4 4.7 %collective-permute-start.40 = (f32[48,128]{1,0:T(8,128)S(1)}, f32[48,128]{1,0:T(8,128)S(1)}, u32[]{:S(2)}, u32[]{:S(2)}) collective-permute-start(f32[48,128]{1,0:T(8,128)S(1)} %add_add_fusion.1), channel_id=1, source_target_pairs={{0,16},{1,17},{2,18},{3,19},{4,20},{5,21},{6,22},{7,23},{8,24},{9,... | collective-permute-start | bytes 73736 | tf_op jit(solution)/shard_map/ppermute | solution.py:1102
  181.2 5.6 %collective-permute-start.41 = (f32[48,128]{1,0:T(8,128)S(1)}, f32[48,128]{1,0:T(8,128)S(1)}, u32[]{:S(2)}, u32[]{:S(2)}) collective-permute-start(f32[48,128]{1,0:T(8,128)S(1)} %add_add_fusion.1), channel_id=1, source_target_pairs={{0,24},{1,25},{2,26},{3,27},{4,28},{5,29},{6,30},{7,31},{8,16},{9,... | collective-permute-start | bytes 73736 | tf_op jit(solution)/shard_map/ppermute | solution.py:1102
  (8 other events, 21.6 us)
